TPU v7x, 512 devices: a whole 4x8x8 slice. The times are simulated.
512 devices in a mesh: tile: 64 (over x, z, y_hi), mode: 8 (over y_lo, core).
Axes of the slice: x: 4, y: 8 (y_hi: 2, y_lo: 4; y = y_hi * 4 + y_lo), z: 8, core: 2. Of those that a mesh axis runs over, the one named last changes fastest.
Arguments:
- object_field: float32 [2, 16384, 768], P(None, 'tile'), may hold values from -5 to 5
- probe_modes: float32 [8, 2, 256, 256], P('mode'), may hold values from -5 to 5
- measured: bfloat16 [256, 256, 256], P('tile'), may hold values from 0.25 to 24
- offsets: int32 [256, 2], P('tile'), may hold values from 0 to 512, as said below
- counts: int32 [64], P('tile'), may hold values from 1 to 4, as said below
Outputs:
- object_grad: float32 [2, 16384, 768], P(None, ('tile', 'mode'))
- probe_grad: float32 [8, 2, 256, 256], P('mode')
Inputs may be any that keep to these rules, and one draw needn't show every extreme that they name: `offsets`: row corners run from 0 to 256 and column corners from 0 to 512; a window's rows past its strip continue into the next strip, after the last strip into the first. Slot 0 of strip 0 has row 256 and column 512. A strip's live slots are its first counts[t]; some strip uses all 4.
All inputs are finite; a program needn't handle non-finite values.
Results may differ from a plain program's by a relative error of at most 0.0003.
Values sent between devices are 32-bit elements; how exact they have to be, the bound alone decides.
A program may use at most 64 MiB of HBM per device.

v0:
```python
import math

import jax
import jax.numpy as jnp
from jax import lax
from jax.sharding import PartitionSpec as P

HIGHEST = lax.Precision.HIGHEST


def from_behind(value, axis, steps):
    count = lax.axis_size(axis)
    pairs = [(source, (source + steps) % count) for source in range(count)]
    return lax.ppermute(value, axis, pairs)


def dft_tables(length):
    grid_index = jnp.arange(length, dtype=jnp.int32)
    product = grid_index[:, None] * grid_index[None, :] % length
    angles = product.astype(jnp.float32) * (2.0 * math.pi / length)
    norm_scale = 1.0 / math.sqrt(length)
    return (jnp.cos(angles) * norm_scale, -jnp.sin(angles) * norm_scale)


def left_apply(table, stack):
    return jnp.einsum("jk,skl->sjl", table, stack, precision=HIGHEST)


def right_apply(stack, table):
    return jnp.einsum("sjk,kl->sjl", stack, table, precision=HIGHEST)


def transform(real_part, imag_part, cos_table, sin_table):
    mid_real = left_apply(cos_table, real_part) - left_apply(sin_table, imag_part)
    mid_imag = left_apply(cos_table, imag_part) + left_apply(sin_table, real_part)
    out_real = right_apply(mid_real, cos_table) - right_apply(mid_imag, sin_table)
    out_imag = right_apply(mid_imag, cos_table) + right_apply(mid_real, sin_table)
    return (out_real, out_imag)


def body(object_field, probe_modes, measured, offsets, counts):
    strip_rows = object_field.shape[1]
    patch_size = probe_modes.shape[2]
    slot_count = measured.shape[0]
    below_rows = from_behind(object_field, "tile", -1)
    extended = jnp.concatenate([object_field, below_rows], axis=1)

    def cut_window(placed):
        return lax.dynamic_slice(
            extended, (jnp.int32(0), placed[0], placed[1]), (2, patch_size, patch_size)
        )

    windows = jax.vmap(cut_window)(offsets)
    win_real = windows[:, 0]
    win_imag = windows[:, 1]
    mode_real = probe_modes[0, 0]
    mode_imag = probe_modes[0, 1]
    wave_real = mode_real * win_real - mode_imag * win_imag
    wave_imag = mode_real * win_imag + mode_imag * win_real
    cos_table, sin_table = dft_tables(patch_size)
    far_real, far_imag = transform(wave_real, wave_imag, cos_table, sin_table)
    own_power = far_real * far_real + far_imag * far_imag
    amplitudes = jnp.sqrt(measured.astype(jnp.float32))
    live_mask = (jnp.arange(slot_count, dtype=jnp.int32) < counts[0]).astype(jnp.float32)[
        :, None, None
    ]
    intensity = lax.psum(own_power, "mode")
    scaling = live_mask * (1.0 - amplitudes / jnp.sqrt(jnp.maximum(intensity, 1.0)))
    back_real, back_imag = transform(scaling * far_real, scaling * far_imag, cos_table, -sin_table)
    grad_real = mode_real * back_real + mode_imag * back_imag
    grad_imag = mode_real * back_imag - mode_imag * back_real
    probe_real = jnp.sum(win_real * back_real + win_imag * back_imag, axis=0)
    probe_imag = jnp.sum(win_real * back_imag - win_imag * back_real, axis=0)
    probe_total = lax.psum(jnp.stack([probe_real, probe_imag]), "tile")
    object_terms = jnp.stack([grad_real, grad_imag], axis=1)
    accumulated = jnp.zeros_like(extended)
    for slot_index in range(slot_count):
        corner = (jnp.int32(0), offsets[slot_index, 0], offsets[slot_index, 1])
        current = lax.dynamic_slice(accumulated, corner, (2, patch_size, patch_size))
        accumulated = lax.dynamic_update_slice(
            accumulated, current + object_terms[slot_index], corner
        )
    own_rows = accumulated[:, :strip_rows]
    spill_part = accumulated[:, strip_rows:]
    arriving = from_behind(spill_part, "tile", 1)
    my_rows = lax.psum_scatter(own_rows + arriving, "mode", scatter_dimension=1, tiled=True)
    return (my_rows, probe_total[None])


def solution(mesh):
    return jax.shard_map(
        body,
        mesh=mesh,
        in_specs=(
            P(None, "tile", None),
            P("mode", None, None, None),
            P("tile", None, None),
            P("tile", None),
            P("tile"),
        ),
        out_specs=(P(None, ("tile", "mode"), None), P("mode", None, None, None)),
        check_vma=False,
    )
```

profile of v0, /device:TPU:1, one launch (start us, length us, event | category | flops | bytes accessed | tf_op | source)
XLA Modules:
  0.0 1195.4 jit_solution(1053550624876355528)
XLA Ops:
  7.2 19.0 %collective-permute-start = (f32[2,256,768]{2,1,0:T(8,128)}, f32[2,256,768]{2,1,0:T(8,128)}, u32[]{:S(2)}, u32[]{:S(2)}) collective-permute-start(f32[2,256,768]{2,1,0:T(8,128)} %param.5), channel_id=1, source_target_pairs={{0,504},{8,0},{16,8},{24,16},{32,24},{40,32},{48,40},{56,48},{64,5... | collective-permute-start | bytes 4718600 | tf_op jit(solution)/shard_map/ppermute | solution.py:14
  28.3 65.1 %collective-permute-done = f32[2,256,768]{2,1,0:T(8,128)} collective-permute-done((f32[2,256,768]{2,1,0:T(8,128)}, f32[2,256,768]{2,1,0:T(8,128)}, u32[]{:S(2)}, u32[]{:S(2)}) %collective-permute-start) | collective-permute-done | bytes 1572896 | tf_op jit(solution)/shard_map/ppermute | solution.py:14
  93.4 3.7 pad_maximum_fusion
  97.1 13.2 %while.1 = (s32[]{:T(128)}, f32[2,512,768]{2,1,0:T(8,128)}, s32[4,3]{1,0:T(4,128)S(1)}, f32[4,2,256,256]{3,2,0,1:T(8,128)S(1)}, s32[]{:T(128)}) while((s32[]{:T(128)}, f32[2,512,768]{2,1,0:T(8,128)}, s32[4,3]{1,0:T(4,128)S(1)}, f32[4,2,256,256]{3,2,0,1:T(8,128)S(1)}, s32[]{:T(128)}) %tuple.38), condition=%wide.while_cond, body=%wide.while_body.sunk | while | flops 2 | bytes 1048701 | solution.py:49
  101.0 2.6 bitcast_dynamic-update-slice_fusion.2
  110.3 2.7 fusion.49
  113.0 2.7 fusion.45
  115.8 2.7 fusion.3
  118.5 2.7 fusion.47
  121.2 2.9 fusion.2
  124.2 2.7 fusion.43
  126.9 2.7 convolution_subtract_fusion.2
  129.7 4.1 multiply_add_fusion
  150.4 60.4 %all-reduce.3.cloned.1.call-done = f32[4,256,256]{2,1,0:T(8,128)} async-done(((f32[4,256,256]{2,1,0:T(8,128)}), f32[4,256,256]{2,1,0:T(8,128)}) %all-reduce.3.cloned.1.call-update) | async-done | bytes 1048592 | tf_op jit(solution)/shard_map/psum | solution.py:67
  210.9 4.4 fusion.24
  215.3 4.3 fusion.1
  219.6 2.7 fusion.40
  222.3 3.5 fusion.20
  225.8 3.1 fusion
  228.9 2.7 fusion.37
  231.6 2.7 convolution_add_fusion
  234.3 4.1 fusion.7
  240.3 3.8 dynamic_update_slice.12
  245.5 6.3 dynamic_update_slice.13
  253.2 6.5 dynamic_update_slice.14
  261.0 6.3 dynamic_update_slice.15
  267.3 2.8 slice.102
  270.1 9.0 collective-permute-start.1
  280.9 72.3 %collective-permute-done.1 = f32[2,256,768]{2,1,0:T(8,128)} collective-permute-done((f32[2,256,768]{2,1,0:T(8,128)}, f32[2,256,768]{2,1,0:T(8,128)}, u32[]{:S(2)}, u32[]{:S(2)}) %collective-permute-start.1) | collective-permute-done | bytes 1572896 | tf_op jit(solution)/shard_map/ppermute | solution.py:14
  353.2 2.8 slice_add_fusion
  356.0 750.1 %all-reduce.5.cloned.1.call-done = f32[1,2,256,256]{3,2,1,0:T(8,128)} async-done(((f32[1,2,256,256]{3,2,1,0:T(8,128)}), f32[1,2,256,256]{3,2,1,0:T(8,128)}) %all-reduce.5.cloned.1.call-update) | async-done | bytes 524304 | tf_op jit(solution)/shard_map/psum | solution.py:74
  1106.1 80.8 %reduce-scatter.2.cloned.1.call-done = f32[2,32,768]{2,1,0:T(8,128)} async-done(((f32[2,256,768]{2,1,0:T(8,128)}), f32[2,32,768]{2,1,0:T(8,128)}) %reduce-scatter.2.cloned.1.call-update) | async-done | bytes 196624 | tf_op jit(solution)/shard_map/reduce_scatter | solution.py:86
  (48 shorter events, 23.2 us)
Async XLA Ops:
  7.2 203.7 %all-reduce.3.cloned.1.call-start = ((), (), s32[]{:S(2)}) async-start(), calls=%async_computation.1 | async-start | bytes 2097152 | tf_op jit(solution)/shard_map/psum | solution.py:67
  7.2 86.2 %collective-permute-start = (f32[2,256,768]{2,1,0:T(8,128)}, f32[2,256,768]{2,1,0:T(8,128)}, u32[]{:S(2)}, u32[]{:S(2)}) collective-permute-start(f32[2,256,768]{2,1,0:T(8,128)} %param.5), channel_id=1, source_target_pairs={{0,504},{8,0},{16,8},{24,16},{32,24},{40,32},{48,40},{56,48},{64,5... | collective-permute-start | bytes 4718600 | tf_op jit(solution)/shard_map/ppermute | solution.py:14
  110.3 11.0 copy-start.2
  129.6 4.4 copy-start.6
  129.6 81.2 %copy-start.5 = (bf16[4,256,256]{2,1,0:T(8,128)(2,1)S(1)}, bf16[4,256,256]{2,1,0:T(8,128)(2,1)}, u32[]{:S(2)}) copy-start(bf16[4,256,256]{2,1,0:T(8,128)(2,1)} %param.7) | copy-start | bytes 1572868
  133.8 972.3 %all-reduce.5.cloned.1.call-start = ((), (), s32[]{:S(2)}) async-start(), calls=%async_computation.3 | async-start | bytes 1048576 | tf_op jit(solution)/shard_map/psum | solution.py:74
  210.9 4.4 copy-start.1
  219.6 2.7 copy-start.4
  231.6 2.7 copy-start.3
  267.3 86.0 %copy-start = (f32[2,512,768]{2,1,0:T(8,128)S(1)}, f32[2,512,768]{2,1,0:T(8,128)}, u32[]{:S(2)}) copy-start(f32[2,512,768]{2,1,0:T(8,128)} %dynamic_update_slice.15) | copy-start | bytes 9437188
  270.1 83.1 %collective-permute-start.1 = (f32[2,256,768]{2,1,0:T(8,128)}, f32[2,256,768]{2,1,0:T(8,128)}, u32[]{:S(2)}, u32[]{:S(2)}) collective-permute-start(f32[2,256,768]{2,1,0:T(8,128)} %slice.102), channel_id=1, source_target_pairs={{0,8},{8,16},{16,24},{24,32},{32,40},{40,48},{48,56},{56,64},{64,7... | collective-permute-start | bytes 4718600 | tf_op jit(solution)/shard_map/ppermute | solution.py:14
  280.9 906.0 %reduce-scatter.2.cloned.1.call-start = ((), (), s32[]{:S(2)}) async-start(), calls=%async_computation.2 | async-start | bytes 1769472 | tf_op jit(solution)/shard_map/reduce_scatter | solution.py:86
Sparse Core Ops, SparseCore 0:
  133.9 76.9 all-reduce.2
  281.0 825.0 all-reduce.4
  1109.8 77.0 reduce-scatter.1
where the time goes:
time: 1210 us; the launch traced here: 1200 us
  waiting for transfers between devices  1030 us (85%)
  matrix products  50.8 us (4%)
  local copies, waits for them, and re-layouts  45.2 us (4%)
  between operations  29.9 us (2%)
  starting transfers between devices  28.3 us (2%)
  other arithmetic  12.4 us (1%)
    psum x1, waiting for transfers between devices, body(): probe_total = lax.psum(jnp.stack([probe_real, probe_imag]), 'tile')  750 us
    ppermute x2, waiting for transfers between devices, from_behind(): return lax.ppermute(value, axis, pairs)  137 us
    reduce_scatter x1, waiting for transfers between devices, body(): lax.psum_scatter(own_rows + arriving, 'mode', scatter_dimension=1, tiled=...  80.8 us
    psum x1, waiting for transfers between devices, body(): intensity = lax.psum(own_power, 'mode')  60.4 us
    ppermute x2, starting transfers between devices, from_behind(): return lax.ppermute(value, axis, pairs)  27.9 us
    dot_general x8, matrix products, left_apply(): return jnp.einsum('jk,skl->sjl', table, stack, precision=HIGHEST)  26.4 us
    dot_general x8, matrix products, right_apply(): return jnp.einsum('sjk,kl->sjl', stack, table, precision=HIGHEST)  24.4 us
  transfers between devices with their start and end apart: 5, of which 5 were waited for; matrix products, arithmetic and copies ran while one was open for 1% of the time, Pallas kernels for 0%

commit v1 on v0

v1 whole, which is shorter than its diff:
```python
import functools
import math

import jax
import jax.numpy as jnp
import numpy as np
from jax import lax
from jax.experimental import pallas as pl
from jax.experimental.pallas import tpu as pltpu
from jax.sharding import PartitionSpec as P

MESH = pl.DeviceIdType.MESH
F32 = jnp.float32
BF16 = jnp.bfloat16
VMEM = pl.BlockSpec(memory_space=pltpu.VMEM)
SMEM = pl.BlockSpec(memory_space=pltpu.SMEM)
ANY = pl.BlockSpec(memory_space=pl.ANY)
LIMIT = 56 * 1024 * 1024
PATCH = 256
STRIP = 256
WIDTH = 768
CAP = 4
CHIPS = 4
TALL, BROAD = PATCH + 8, PATCH + 128
PAIR = 2

HALO_CUTS = 4
SUM_CUTS = 4


def place():
    tile, mode = lax.axis_index("tile"), lax.axis_index("mode")
    return tile, mode, mode // 2, mode % 2


def ring_ends(tiles, tile, mode, chip, core):
    after = lax.rem(tile + 1, tiles)
    before = lax.rem(tile + tiles - 1, tiles)
    return dict(
        above=(jnp.where(chip < 3, tile, after), jnp.where(chip < 3, mode + 2, core)),
        below=(jnp.where(chip > 0, tile, after), jnp.where(chip > 0, mode - 2, core + 6)),
        to_below=(jnp.where(chip > 0, tile, before), jnp.where(chip > 0, mode - 2, core + 6)),
        to_above=(jnp.where(chip < 3, tile, before), jnp.where(chip < 3, mode + 2, core)),
    )


def greet(devices):
    barrier = pltpu.get_barrier_semaphore()
    for device in devices:
        pl.semaphore_signal(barrier, inc=1, device_id=device, device_id_type=MESH)
    pl.semaphore_wait(barrier, len(devices))


def remote(source, target, send_sem, recv_sem, device):
    return pltpu.make_async_remote_copy(
        src_ref=source, dst_ref=target, send_sem=send_sem, recv_sem=recv_sem, device_id=device, device_id_type=MESH
    )


def halo_kernel(tiles, object_ref, probe_ref, ext_ref, modes_ref, own_sem, probe_sem, probe_send, probe_recv,
                chain_send, chain_recv, pair_send, pair_recv):
    tile, mode, chip, core = place()
    sibling = (tile, mode + 1 - 2 * core)
    ends = ring_ends(tiles, tile, mode, chip, core)
    own_copy = pltpu.make_async_copy(object_ref, ext_ref.at[:, pl.ds(0, STRIP)], own_sem)
    own_copy.start()
    probe_copy = pltpu.make_async_copy(probe_ref.at[0], modes_ref.at[core], probe_sem)
    probe_copy.start()
    greet([ends["above"], ends["below"], ends["to_above"], ends["to_below"], sibling])
    swap = remote(probe_ref.at[0], modes_ref.at[core], probe_send, probe_recv, sibling)
    swap.start()
    own_copy.wait()

    depth = STRIP // 4 // HALO_CUTS
    targets = (ends["to_below"], ends["to_above"])
    passes_on = (chip > 0, chip < 3)

    def rows(way, cut):
        return (2 * way + core) * (STRIP // 4) + cut * depth

    def chain(way, cut, base):
        row = rows(way, cut)
        return remote(
            ext_ref.at[:, pl.ds(base + row, depth)],
            ext_ref.at[:, pl.ds(STRIP + row, depth)],
            chain_send.at[way, cut],
            chain_recv.at[way, cut],
            targets[way],
        )

    def across(way, cut):
        block = ext_ref.at[:, pl.ds(STRIP + rows(way, cut), depth)]
        return remote(block, block, pair_send.at[way, cut], pair_recv.at[way, cut], sibling)

    for way in range(2):
        @pl.when(jnp.logical_not(passes_on[way]))
        def _():
            for cut in range(HALO_CUTS):
                chain(way, cut, 0).start()

    for cut in range(HALO_CUTS):
        for way in range(2):
            chain(way, cut, 0).wait_recv()
            @pl.when(passes_on[way])
            def _():
                chain(way, cut, STRIP).start()
            across(way, cut).start()

    for cut in range(HALO_CUTS):
        for way in range(2):
            chain(way, cut, 0).wait_send()
            across(way, cut).wait_send()
    for cut in range(HALO_CUTS):
        for way in range(2):
            sent = (2 * way + 1 - core) * (STRIP // 4) + cut * depth
            block = ext_ref.at[:, pl.ds(STRIP + sent, depth)]
            remote(block, block, pair_send.at[way, cut], pair_recv.at[way, cut], sibling).wait_recv()
    swap.wait()
    probe_copy.wait()


def halo(tiles, object_field, probe_modes):
    return pl.pallas_call(
        functools.partial(halo_kernel, tiles),
        out_shape=(
            jax.ShapeDtypeStruct((2, 2 * STRIP, WIDTH), F32),
            jax.ShapeDtypeStruct((PAIR, 2, PATCH, PATCH), F32),
        ),
        in_specs=[ANY, VMEM],
        out_specs=(VMEM, VMEM),
        scratch_shapes=[
            pltpu.SemaphoreType.DMA,
            pltpu.SemaphoreType.DMA,
            pltpu.SemaphoreType.DMA,
            pltpu.SemaphoreType.DMA,
            pltpu.SemaphoreType.DMA((2, HALO_CUTS)),
            pltpu.SemaphoreType.DMA((2, HALO_CUTS)),
            pltpu.SemaphoreType.DMA((2, HALO_CUTS)),
            pltpu.SemaphoreType.DMA((2, HALO_CUTS)),
        ],
        compiler_params=pltpu.CompilerParams(collective_id=0, has_side_effects=True, vmem_limit_bytes=LIMIT),
        name="halo",
    )(object_field, probe_modes)


def split(value):
    high = value.astype(BF16)
    return high, (value - high.astype(F32)).astype(BF16)


def dft_tables():
    index = np.arange(PATCH)
    angle = 2.0 * math.pi * ((index[:, None] * index[None, :]) % PATCH) / PATCH
    cos, sin = np.cos(angle) / math.sqrt(PATCH), np.sin(angle) / math.sqrt(PATCH)

    def parts(block):
        high = block.astype(jnp.bfloat16)
        low = (block - high.astype(np.float64)).astype(jnp.bfloat16)
        return high, low

    tables = []
    for sine in (-sin, sin):
        high, low = parts(np.block([[cos, -sine], [sine, cos]]))
        tables.append(np.concatenate([high, high, low], axis=1))
        high, low = parts(np.block([[cos, sine], [-sine, cos]]))
        tables.append(np.concatenate([high, high, low], axis=0))
    return tables


def transform(real, imag, left_ref, right_ref):
    high, low = split(jnp.concatenate([real, imag], axis=0))
    mid = jnp.dot(left_ref[...], jnp.concatenate([high, low, high], axis=0), preferred_element_type=F32)
    high, low = split(jnp.concatenate([mid[:PATCH], mid[PATCH:]], axis=1))
    out = jnp.dot(jnp.concatenate([high, low, high], axis=1), right_ref[...], preferred_element_type=F32)
    return out[:, :PATCH], out[:, PATCH:]


def corner(offsets_ref, slot):
    row, column = offsets_ref[slot, 0], offsets_ref[slot, 1]
    top = jnp.minimum(row // 8, (2 * STRIP - TALL) // 8) * 8
    left = jnp.minimum(column // 128, (WIDTH - BROAD) // 128) * 128
    return pl.ds(pl.multiple_of(top, 8), TALL), pl.ds(pl.multiple_of(left, 128), BROAD), row - top, column - left


def forward_kernel(ext_ref, modes_ref, offsets_ref, left_ref, right_ref, windows_ref, far_ref, power_ref):
    core = lax.axis_index("mode") % 2
    for local in range(2):
        rows, columns, down, right = corner(offsets_ref, 2 * core + local)
        window = []
        for part in range(2):
            block = pltpu.roll(ext_ref[part, rows, columns], lax.rem(BROAD - right, BROAD), 1)[:, :PATCH]
            block = pltpu.roll(block, lax.rem(TALL - down, TALL), 0)[:PATCH]
            windows_ref[local, part] = block
            window.append(block)
        for pair in range(PAIR):
            mode_real, mode_imag = modes_ref[pair, 0], modes_ref[pair, 1]
            far_real, far_imag = transform(
                mode_real * window[0] - mode_imag * window[1],
                mode_real * window[1] + mode_imag * window[0],
                left_ref,
                right_ref,
            )
            far_ref[local, pair, 0] = far_real
            far_ref[local, pair, 1] = far_imag
            power = far_real * far_real + far_imag * far_imag
            if pair == 0:
                power_ref[local] = power
            else:
                power_ref[local] += power


def forward(ext, modes, offsets, left, right):
    return pl.pallas_call(
        forward_kernel,
        out_shape=(
            jax.ShapeDtypeStruct((2, 2, PATCH, PATCH), F32),
            jax.ShapeDtypeStruct((2, PAIR, 2, PATCH, PATCH), F32),
            jax.ShapeDtypeStruct((2, PATCH, PATCH), F32),
        ),
        in_specs=[VMEM, VMEM, SMEM, VMEM, VMEM],
        out_specs=(VMEM, VMEM, VMEM),
        compiler_params=pltpu.CompilerParams(vmem_limit_bytes=LIMIT),
        name="forward",
    )(ext, modes, offsets, left, right)


def sum_kernel(power_ref, total_ref, staged, arrived, send_sem, recv_sem):
    tile, mode, chip, core = place()
    lower, upper = (tile, mode - 2), (tile, mode + 2)
    has_lower, has_upper = chip > 0, chip < CHIPS - 1
    barrier = pltpu.get_barrier_semaphore()
    for there, device in ((has_lower, lower), (has_upper, upper)):
        @pl.when(there)
        def _():
            pl.semaphore_signal(barrier, inc=1, device_id=device, device_id_type=MESH)
    pl.semaphore_wait(barrier, has_lower.astype(jnp.int32) + has_upper.astype(jnp.int32))

    depth = 2 * PATCH // SUM_CUTS

    def block(cut):
        return pl.ds(cut * depth, depth)

    ways = ((has_lower, has_upper, upper), (has_upper, has_lower, lower))

    def hop(way, cut, source):
        return remote(
            source.at[block(cut)], arrived.at[way, block(cut)], send_sem.at[way, cut], recv_sem.at[way, cut], ways[way][2]
        )

    for way, (hears, sends, _) in enumerate(ways):
        @pl.when(jnp.logical_not(hears))
        def _():
            for cut in range(SUM_CUTS):
                hop(way, cut, power_ref).start()

    for cut in range(SUM_CUTS):
        for way, (hears, sends, _) in enumerate(ways):
            @pl.when(hears)
            def _():
                hop(way, cut, power_ref).wait_recv()

            @pl.when(jnp.logical_and(hears, sends))
            def _():
                staged[way, block(cut)] = power_ref[block(cut)] + arrived[way, block(cut)]
                hop(way, cut, staged.at[way]).start()
        rows = block(cut)

        @pl.when(jnp.logical_not(has_lower))
        def _():
            total_ref[rows] = power_ref[rows] + arrived[1, rows]

        @pl.when(jnp.logical_not(has_upper))
        def _():
            total_ref[rows] = power_ref[rows] + arrived[0, rows]

        @pl.when(jnp.logical_and(has_lower, has_upper))
        def _():
            total_ref[rows] = power_ref[rows] + (arrived[0, rows] + arrived[1, rows])

    for way, (hears, sends, _) in enumerate(ways):
        @pl.when(sends)
        def _():
            for cut in range(SUM_CUTS):
                hop(way, cut, power_ref).wait_send()


def sum_power(power):
    rows = 2 * PATCH
    return pl.pallas_call(
        sum_kernel,
        out_shape=jax.ShapeDtypeStruct((rows, PATCH), F32),
        in_specs=[VMEM],
        out_specs=VMEM,
        scratch_shapes=[
            pltpu.VMEM((2, rows, PATCH), F32),
            pltpu.VMEM((2, rows, PATCH), F32),
            pltpu.SemaphoreType.DMA((2, SUM_CUTS)),
            pltpu.SemaphoreType.DMA((2, SUM_CUTS)),
        ],
        compiler_params=pltpu.CompilerParams(collective_id=1, has_side_effects=True, vmem_limit_bytes=LIMIT),
        name="sum_power",
    )(power.reshape(rows, PATCH)).reshape(2, PATCH, PATCH)


def back_kernel(total_ref, far_ref, windows_ref, modes_ref, measured_ref, offsets_ref, counts_ref, left_ref, right_ref,
                acc_ref, probe_ref):
    core = lax.axis_index("mode") % 2
    acc_ref[...] = jnp.zeros_like(acc_ref)
    for local in range(2):
        slot = 2 * core + local
        amplitude = jnp.sqrt(measured_ref[slot].astype(F32))
        live = (slot < counts_ref[0]).astype(F32)
        scaling = live * (1.0 - amplitude / jnp.sqrt(jnp.maximum(total_ref[local], 1.0)))
        win_real, win_imag = windows_ref[local, 0], windows_ref[local, 1]
        term_real = term_imag = None
        for pair in range(PAIR):
            back_real, back_imag = transform(
                scaling * far_ref[local, pair, 0], scaling * far_ref[local, pair, 1], left_ref, right_ref
            )
            mode_real, mode_imag = modes_ref[pair, 0], modes_ref[pair, 1]
            grad_real = mode_real * back_real + mode_imag * back_imag
            grad_imag = mode_real * back_imag - mode_imag * back_real
            term_real = grad_real if term_real is None else term_real + grad_real
            term_imag = grad_imag if term_imag is None else term_imag + grad_imag
            probe_real = win_real * back_real + win_imag * back_imag
            probe_imag = win_real * back_imag - win_imag * back_real
            if local == 0:
                probe_ref[pair, 0] = probe_real
                probe_ref[pair, 1] = probe_imag
            else:
                probe_ref[pair, 0] += probe_real
                probe_ref[pair, 1] += probe_imag
        rows, columns, down, right = corner(offsets_ref, slot)
        for part, term in enumerate((term_real, term_imag)):
            term = jnp.concatenate([term, jnp.zeros((TALL - PATCH, PATCH), F32)], axis=0)
            term = jnp.concatenate([pltpu.roll(term, down, 0), jnp.zeros((TALL, BROAD - PATCH), F32)], axis=1)
            acc_ref[part, rows, columns] += pltpu.roll(term, right, 1)


def back(total, far, windows, modes, measured, offsets, counts, left, right):
    return pl.pallas_call(
        back_kernel,
        out_shape=(
            jax.ShapeDtypeStruct((2, 2 * STRIP, WIDTH), F32),
            jax.ShapeDtypeStruct((PAIR, 2, PATCH, PATCH), F32),
        ),
        in_specs=[VMEM, VMEM, VMEM, VMEM, VMEM, SMEM, SMEM, VMEM, VMEM],
        out_specs=(VMEM, VMEM),
        compiler_params=pltpu.CompilerParams(vmem_limit_bytes=LIMIT),
        name="back",
    )(total, far, windows, modes, measured, offsets, counts, left, right)


def gather_kernel(tiles, grid_x, grid_z, acc_ref, terms_ref, object_ref, probe_ref, pair_buf, up_out, up_in, down_out,
                  down_in, probe_buf, mine, x_in, z_in, pair_send, pair_recv, up_send, up_recv, down_send, down_recv,
                  probe_send, probe_recv, x_send, x_recv, z_send, z_recv, h_send, h_recv, zg_send, zg_recv, xg_send,
                  xg_recv):
    tile, mode, chip, core = place()
    sibling = (tile, mode + 1 - 2 * core)
    after = lax.rem(tile + 1, tiles)
    before = lax.rem(tile + tiles - 1, tiles)
    to_up = (jnp.where(chip < 3, tile, after), jnp.where(chip < 3, mode + 2, core))
    from_up = (jnp.where(chip > 0, tile, before), jnp.where(chip > 0, mode - 2, core + 6))
    to_down = (jnp.where(chip > 0, tile, after), jnp.where(chip > 0, mode - 2, core + 6))
    from_down = (jnp.where(chip < 3, tile, before), jnp.where(chip < 3, mode + 2, core))

    high, plane = tile % 2, tile // 2
    at_z, at_x = plane % grid_z, plane // grid_z

    def at(x, z, h):
        return ((x * grid_z + z) * 2 + h, mode)

    x_peers = [lax.rem(at_x + step, grid_x) for step in range(1, grid_x)]
    z_peers = [lax.rem(at_z + step, grid_z) for step in range(1, grid_z)]
    x_ids = [at(peer, at_z, high) for peer in x_peers]
    z_ids = [at(at_x, peer, high) for peer in z_peers]
    h_id = at(at_x, at_z, 1 - high)
    greet([to_up, from_up, to_down, from_down, sibling, h_id] + x_ids + z_ids)

    probe_pair = remote(terms_ref.at[1 - core], probe_buf, probe_send, probe_recv, sibling)
    probe_pair.start()

    def pair_copy(block):
        return remote(
            acc_ref.at[:, 2 * block + 1 - core], pair_buf.at[:, block], pair_send.at[block], pair_recv.at[block], sibling
        )

    pair_order = (4, 7, 5, 6, 3, 0, 2, 1)
    for block in pair_order:
        pair_copy(block).start()

    ready = set()

    def part(block):
        if block not in ready:
            ready.add(block)
            pair_copy(block).wait()
            pair_buf[:, block] += acc_ref[:, 2 * block + core]
        return pair_buf[:, block]

    depth_x = 2 * PATCH // grid_x
    depth_z = depth_x // grid_z
    probe_pair.wait()
    mine[...] = probe_buf[...] + terms_ref[core]

    def x_copy(step):
        peer = x_peers[step]
        return remote(
            mine.at[pl.ds(peer * depth_x, depth_x)], x_in.at[step], x_send.at[step], x_recv.at[step], x_ids[step]
        )

    for step in range(grid_x - 1):
        x_copy(step).start()

    def up_copy(item):
        return remote(up_out.at[item], up_in.at[item], up_send.at[item], up_recv.at[item], to_up)

    def down_copy(item):
        return remote(down_out.at[item], down_in.at[item], down_send.at[item], down_recv.at[item], to_down)

    chains = (
        (up_copy, up_out, up_in, chip, (4, 5, 3, 2, 1)),
        (down_copy, down_out, down_in, CHIPS - 1 - chip, (7, 6, 0, 1, 2)),
    )

    for block in pair_order:
        part(block)

    def advance(way, item):
        copy, out, arrived, rank, blocks = chains[way]
        block = blocks[item]
        if item < 2:
            @pl.when(rank == 0)
            def _():
                out[item] = pair_buf[:, block]

            @pl.when(rank > 0)
            def _():
                copy(item).wait_recv()
                out[item] = pair_buf[:, block] + arrived[item]

            copy(item).start()
        else:
            last = 5 - item
            if item < 4:
                @pl.when(rank == 0)
                def _():
                    out[item] = pair_buf[:, block]
                    copy(item).start()

                @pl.when(jnp.logical_and(rank > 0, rank < last))
                def _():
                    copy(item).wait_recv()
                    out[item] = pair_buf[:, block] + arrived[item]
                    copy(item).start()
            else:
                @pl.when(rank == 0)
                def _():
                    copy(1).wait_recv()
                    out[item] = pair_buf[:, block] + arrived[1]
                    copy(item).start()

    for item in range(4):
        advance(0, item)
        advance(1, item)

    for step in range(grid_x - 1):
        x_copy(step).wait()
    own_x = pl.ds(at_x * depth_x, depth_x)
    total = mine[own_x]
    for step in range(grid_x - 1):
        total = total + x_in[step]
    mine[own_x] = total

    def z_copy(step):
        peer = z_peers[step]
        return remote(
            mine.at[pl.ds(at_x * depth_x + peer * depth_z, depth_z)],
            z_in.at[step],
            z_send.at[step],
            z_recv.at[step],
            z_ids[step],
        )

    for step in range(grid_z - 1):
        z_copy(step).start()
    for step in range(grid_z - 1):
        z_copy(step).wait()
    own_z = pl.ds(at_x * depth_x + at_z * depth_z, depth_z)
    total = mine[own_z]
    for step in range(grid_z - 1):
        total = total + z_in[step]
    mine[own_z] = total

    h_copy = remote(mine.at[own_z], z_in.at[grid_z - 1], h_send, h_recv, h_id)
    h_copy.start()
    for way in range(2):
        advance(way, 4)
    h_copy.wait()
    probe_ref[own_z] = mine[own_z] + z_in[grid_z - 1]

    def z_back(step, owner):
        rows = pl.ds(at_x * depth_x + owner * depth_z, depth_z)
        return remote(probe_ref.at[rows], probe_ref.at[rows], zg_send.at[step], zg_recv.at[step], z_ids[step])

    for step in range(grid_z - 1):
        z_back(step, at_z).start()
    for step in range(grid_z - 1):
        z_back(step, at_z).wait_send()
        sender = lax.rem(at_z + grid_z - step - 1, grid_z)
        z_back(step, sender).wait_recv()

    def x_back(step, owner):
        rows = pl.ds(owner * depth_x, depth_x)
        return remote(probe_ref.at[rows], probe_ref.at[rows], xg_send.at[step], xg_recv.at[step], x_ids[step])

    for step in range(grid_x - 1):
        x_back(step, at_x).start()

    for chip_at in range(CHIPS):
        @pl.when(chip == chip_at)
        def _():
            result = pair_buf[:, chip_at]
            for way in range(2):
                copy, out, arrived, rank, blocks = chains[way]
                here = chip_at if way == 0 else CHIPS - 1 - chip_at
                if here == 0:
                    copy(0).wait_recv()
                    result = result + arrived[0]
                else:
                    copy(5 - here).wait_recv()
                    result = result + arrived[5 - here]
            object_ref[...] = result

    for way in range(2):
        copy, out, arrived, rank, blocks = chains[way]
        for item in range(5):
            if item < 2:
                copy(item).wait_send()
            else:
                @pl.when(rank < 5 - item)
                def _():
                    copy(item).wait_send()

    for step in range(grid_x - 1):
        x_back(step, at_x).wait_send()
        sender = lax.rem(at_x + grid_x - step - 1, grid_x)
        x_back(step, sender).wait_recv()


def gather(tiles, grid_x, grid_z, acc, terms):
    rows = 2 * PATCH
    depth_x = rows // grid_x
    depth_z = depth_x // grid_z
    block = (2, 32, WIDTH)
    dma = pltpu.SemaphoreType.DMA
    object_rows, probe = pl.pallas_call(
        functools.partial(gather_kernel, tiles, grid_x, grid_z),
        out_shape=(jax.ShapeDtypeStruct(block, F32), jax.ShapeDtypeStruct((rows, PATCH), F32)),
        in_specs=[VMEM, VMEM],
        out_specs=(VMEM, VMEM),
        scratch_shapes=[
            pltpu.VMEM((2, 8, 32, WIDTH), F32),
            pltpu.VMEM((5,) + block, F32),
            pltpu.VMEM((5,) + block, F32),
            pltpu.VMEM((5,) + block, F32),
            pltpu.VMEM((5,) + block, F32),
            pltpu.VMEM((rows, PATCH), F32),
            pltpu.VMEM((rows, PATCH), F32),
            pltpu.VMEM((max(grid_x - 1, 1), depth_x, PATCH), F32),
            pltpu.VMEM((grid_z, depth_z, PATCH), F32),
            dma((8,)), dma((8,)),
            dma((5,)), dma((5,)), dma((5,)), dma((5,)),
            dma, dma,
            dma((max(grid_x - 1, 1),)), dma((max(grid_x - 1, 1),)),
            dma((grid_z,)), dma((grid_z,)),
            dma, dma,
            dma((grid_z,)), dma((grid_z,)),
            dma((max(grid_x - 1, 1),)), dma((max(grid_x - 1, 1),)),
        ],
        compiler_params=pltpu.CompilerParams(collective_id=2, has_side_effects=True, vmem_limit_bytes=LIMIT),
        name="gather",
    )(acc.reshape(2, 16, 32, WIDTH), terms.reshape(PAIR, rows, PATCH))
    return object_rows, probe.reshape(1, 2, PATCH, PATCH)


def solution(mesh):
    tiles = mesh.shape["tile"]
    grid_x = 4 if tiles == 64 else 2
    grid_z = tiles // 2 // grid_x
    left_forward, right_forward, left_back, right_back = dft_tables()

    def body(object_field, probe_modes, measured, offsets, counts):
        ext, modes = halo(tiles, object_field, probe_modes)
        windows, far, power = forward(ext, modes, offsets, jnp.asarray(left_forward), jnp.asarray(right_forward))
        total = sum_power(power)
        acc, terms = back(
            total, far, windows, modes, measured, offsets, counts, jnp.asarray(left_back), jnp.asarray(right_back)
        )
        return gather(tiles, grid_x, grid_z, acc, terms)

    return jax.shard_map(
        body,
        mesh=mesh,
        in_specs=(
            P(None, "tile", None),
            P("mode", None, None, None),
            P("tile", None, None),
            P("tile", None),
            P("tile"),
        ),
        out_specs=(P(None, ("tile", "mode"), None), P("mode", None, None, None)),
        check_vma=False,
    )
```

time: 1210 us -> 287 us (0.24)
  the two profiles are of different devices: /device:TPU:1 before, /device:TPU:8 now
where the time goes in v1:
time: 287 us
  Pallas kernels  281 us (98%)
  local copies, waits for them, and re-layouts  4.82 us (2%)
    pallas_call x1, Pallas kernels, gather(): pl.pallas_call(functools.partial(gather_kernel, tiles, grid_x, grid_z), o...  116 us
    pallas_call x1, Pallas kernels, halo(): pl.pallas_call(functools.partial(halo_kernel, tiles), out_shape=(jax.Shap...  100 us
    pallas_call x1, Pallas kernels, sum_power(): pl.pallas_call(sum_kernel, out_shape=jax.ShapeDtypeStruct((rows, PATCH),...  44.7 us
    pallas_call x1, Pallas kernels, back(): pl.pallas_call(back_kernel, out_shape=(jax.ShapeDtypeStruct((2, 2 * STRIP...  10.6 us
    pallas_call x1, Pallas kernels, forward(): pl.pallas_call(forward_kernel, out_shape=(jax.ShapeDtypeStruct((2, 2, PAT...  9.44 us

profile of v1, /device:TPU:8, one launch (start us, length us, event | category | flops | bytes accessed | tf_op | source)
XLA Modules:
  0.0 286.9 jit_solution(3123523101199816830)
XLA Ops:
  1.3 1.3 copy.11.offsets_ref
  2.6 100.4 %halo.1 = (f32[2,512,768]{2,1,0:T(8,128)}, f32[2,2,256,256]{3,2,1,0:T(8,128)}) custom-call(f32[2,256,768]{2,1,0:T(8,128)} %object_ref.1, f32[1,2,256,256]{3,2,1,0:T(8,128)} %probe_ref.1), custom_call_target="tpu_custom_call" | custom-call | tf_op jit(solution)/shard_map/halo/pallas_call | solution.py:123
  103.1 9.4 %forward.1 = (f32[2,2,256,256]{3,2,1,0:T(8,128)}, f32[2,2,2,256,256]{4,3,2,1,0:T(8,128)}, f32[2,256,256]{2,1,0:T(8,128)}) custom-call(f32[2,512,768]{2,1,0:T(8,128)} %get-tuple-element.11.ext_ref, f32[2,2,256,256]{3,2,1,0:T(8,128)} %get-tuple-element.12.modes_ref, s32[4,2]{1,0:T(4,128)} %copy.11.offsets_ref, bf16[512,1536]{1,0:T(8,128)(2,1)} %constant.8.clone.left_ref, ...), custom_call_target="tpu_custom_call" | custom-call | tf_op jit(solution)/shard_map/forward/pallas_call | solution.py:213
  112.5 44.7 %sum_power.1 = f32[512,256]{1,0:T(8,128)} custom-call(f32[512,256]{1,0:T(8,128)} %bitcast.8), custom_call_target="tpu_custom_call" | custom-call | tf_op jit(solution)/shard_map/sum_power/pallas_call | solution.py:289
  157.2 10.6 %back.1 = (f32[2,512,768]{2,1,0:T(8,128)}, f32[2,2,256,256]{3,2,1,0:T(8,128)}) custom-call(f32[2,256,256]{2,1,0:T(8,128)} %bitcast.6, f32[2,2,2,256,256]{4,3,2,1,0:T(8,128)} %get-tuple-element.14.far_ref, f32[2,2,256,256]{3,2,1,0:T(8,128)} %get-tuple-element.15.windows_ref, f32[2,2,256,256]{3,2,1,0:T(8,128)} %get-tuple-element.12.modes_ref, ...), custom_call_target="tpu_custom_call" | custom-call | tf_op jit(solution)/shard_map/back/pallas_call | solution.py:341
  167.8 115.6 %gather.1 = (f32[2,32,768]{2,1,0:T(8,128)}, f32[512,256]{1,0:T(8,128)}) custom-call(f32[2,16,32,768]{3,2,1,0:T(8,128)} %bitcast.5, f32[2,512,256]{2,1,0:T(8,128)} %bitcast.7), custom_call_target="tpu_custom_call" | custom-call | tf_op jit(solution)/shard_map/gather/pallas_call | solution.py:557
  283.4 1.6 copy.16
  285.1 1.9 copy.17

commit v2 on v1

--- a/solution.py
+++ b/solution.py
@@ -24,8 +24,9 @@
 TALL, BROAD = PATCH + 8, PATCH + 128
 PAIR = 2
 
-HALO_CUTS = 4
-SUM_CUTS = 4
+HALO_CUTS = 8
+SUM_CUTS = 16
+LATENCY = 2.3
 
 
 def place():
@@ -98,13 +99,19 @@
             for cut in range(HALO_CUTS):
                 chain(way, cut, 0).start()
 
-    for cut in range(HALO_CUTS):
-        for way in range(2):
-            chain(way, cut, 0).wait_recv()
-            @pl.when(passes_on[way])
-            def _():
-                chain(way, cut, STRIP).start()
-            across(way, cut).start()
+    for here in range(CHIPS):
+        @pl.when(chip == here)
+        def _():
+            step = 8.0 / HALO_CUTS
+            events = []
+            for way, rank in ((0, CHIPS - 1 - here), (1, here)):
+                for cut in range(HALO_CUTS):
+                    events.append(((rank + 1) * (step + LATENCY) + cut * step, way, cut, rank < CHIPS - 1))
+            for _, way, cut, forwards in sorted(events):
+                chain(way, cut, 0).wait_recv()
+                if forwards:
+                    chain(way, cut, STRIP).start()
+                across(way, cut).start()
 
     for cut in range(HALO_CUTS):
         for way in range(2):
@@ -253,29 +260,28 @@
             for cut in range(SUM_CUTS):
                 hop(way, cut, power_ref).start()
 
-    for cut in range(SUM_CUTS):
-        for way, (hears, sends, _) in enumerate(ways):
-            @pl.when(hears)
-            def _():
+    for here in range(CHIPS):
+        @pl.when(chip == here)
+        def _():
+            step = 10.5 / SUM_CUTS
+            events = []
+            for way, rank in ((0, here), (1, CHIPS - 1 - here)):
+                if rank > 0:
+                    for cut in range(SUM_CUTS):
+                        events.append((rank * (step + LATENCY) + cut * step, way, cut, rank < CHIPS - 1))
+            seen = [0] * SUM_CUTS
+            for _, way, cut, forwards in sorted(events):
+                rows = block(cut)
                 hop(way, cut, power_ref).wait_recv()
-
-            @pl.when(jnp.logical_and(hears, sends))
-            def _():
-                staged[way, block(cut)] = power_ref[block(cut)] + arrived[way, block(cut)]
-                hop(way, cut, staged.at[way]).start()
-        rows = block(cut)
-
-        @pl.when(jnp.logical_not(has_lower))
-        def _():
-            total_ref[rows] = power_ref[rows] + arrived[1, rows]
-
-        @pl.when(jnp.logical_not(has_upper))
-        def _():
-            total_ref[rows] = power_ref[rows] + arrived[0, rows]
-
-        @pl.when(jnp.logical_and(has_lower, has_upper))
-        def _():
-            total_ref[rows] = power_ref[rows] + (arrived[0, rows] + arrived[1, rows])
+                if forwards:
+                    staged[way, rows] = power_ref[rows] + arrived[way, rows]
+                    hop(way, cut, staged.at[way]).start()
+                seen[cut] += 1
+                if seen[cut] == 1 + (0 < here < CHIPS - 1):
+                    if 0 < here < CHIPS - 1:
+                        total_ref[rows] = power_ref[rows] + (arrived[0, rows] + arrived[1, rows])
+                    else:
+                        total_ref[rows] = power_ref[rows] + arrived[way, rows]
 
     for way, (hears, sends, _) in enumerate(ways):
         @pl.when(sends)
@@ -351,9 +357,8 @@
     )(total, far, windows, modes, measured, offsets, counts, left, right)
 
 
-def gather_kernel(tiles, grid_x, grid_z, acc_ref, terms_ref, object_ref, probe_ref, pair_buf, up_out, up_in, down_out,
-                  down_in, probe_buf, mine, x_in, z_in, pair_send, pair_recv, up_send, up_recv, down_send, down_recv,
-                  probe_send, probe_recv, x_send, x_recv, z_send, z_recv, h_send, h_recv, zg_send, zg_recv, xg_send,
+def gather_kernel(tiles, grid_x, grid_z, acc_ref, terms_ref, object_ref, probe_ref, pair_buf, chain_out, chain_in,
+                  probe_buf, mine, x_in, z_in, pair_send, pair_recv, chain_send, chain_recv, probe_send, probe_recv, x_send, x_recv, z_send, z_recv, h_send, h_recv, zg_send, zg_recv, xg_send,
                   xg_recv):
     tile, mode, chip, core = place()
     sibling = (tile, mode + 1 - 2 * core)
@@ -385,18 +390,9 @@
             acc_ref.at[:, 2 * block + 1 - core], pair_buf.at[:, block], pair_send.at[block], pair_recv.at[block], sibling
         )
 
-    pair_order = (4, 7, 5, 6, 3, 0, 2, 1)
+    pair_order = (5, 6, 4, 7, 3, 0, 2, 1)
     for block in pair_order:
         pair_copy(block).start()
-
-    ready = set()
-
-    def part(block):
-        if block not in ready:
-            ready.add(block)
-            pair_copy(block).wait()
-            pair_buf[:, block] += acc_ref[:, 2 * block + core]
-        return pair_buf[:, block]
 
     depth_x = 2 * PATCH // grid_x
     depth_z = depth_x // grid_z
@@ -412,140 +408,137 @@
     for step in range(grid_x - 1):
         x_copy(step).start()
 
-    def up_copy(item):
-        return remote(up_out.at[item], up_in.at[item], up_send.at[item], up_recv.at[item], to_up)
-
-    def down_copy(item):
-        return remote(down_out.at[item], down_in.at[item], down_send.at[item], down_recv.at[item], to_down)
-
-    chains = (
-        (up_copy, up_out, up_in, chip, (4, 5, 3, 2, 1)),
-        (down_copy, down_out, down_in, CHIPS - 1 - chip, (7, 6, 0, 1, 2)),
-    )
-
-    for block in pair_order:
-        part(block)
-
-    def advance(way, item):
-        copy, out, arrived, rank, blocks = chains[way]
-        block = blocks[item]
-        if item < 2:
-            @pl.when(rank == 0)
-            def _():
-                out[item] = pair_buf[:, block]
-
-            @pl.when(rank > 0)
-            def _():
-                copy(item).wait_recv()
-                out[item] = pair_buf[:, block] + arrived[item]
-
-            copy(item).start()
-        else:
-            last = 5 - item
-            if item < 4:
-                @pl.when(rank == 0)
-                def _():
-                    out[item] = pair_buf[:, block]
-                    copy(item).start()
-
-                @pl.when(jnp.logical_and(rank > 0, rank < last))
-                def _():
-                    copy(item).wait_recv()
-                    out[item] = pair_buf[:, block] + arrived[item]
-                    copy(item).start()
-            else:
-                @pl.when(rank == 0)
-                def _():
-                    copy(1).wait_recv()
-                    out[item] = pair_buf[:, block] + arrived[1]
-                    copy(item).start()
-
-    for item in range(4):
-        advance(0, item)
-        advance(1, item)
-
-    for step in range(grid_x - 1):
-        x_copy(step).wait()
+    def chain_copy(way, item):
+        return remote(
+            chain_out.at[way, item], chain_in.at[way, item], chain_send.at[way, item], chain_recv.at[way, item],
+            (to_up, to_down)[way],
+        )
+
     own_x = pl.ds(at_x * depth_x, depth_x)
-    total = mine[own_x]
-    for step in range(grid_x - 1):
-        total = total + x_in[step]
-    mine[own_x] = total
+    own_z = pl.ds(at_x * depth_x + at_z * depth_z, depth_z)
 
     def z_copy(step):
-        peer = z_peers[step]
-        return remote(
-            mine.at[pl.ds(at_x * depth_x + peer * depth_z, depth_z)],
-            z_in.at[step],
-            z_send.at[step],
-            z_recv.at[step],
-            z_ids[step],
-        )
-
-    for step in range(grid_z - 1):
-        z_copy(step).start()
-    for step in range(grid_z - 1):
-        z_copy(step).wait()
-    own_z = pl.ds(at_x * depth_x + at_z * depth_z, depth_z)
-    total = mine[own_z]
-    for step in range(grid_z - 1):
-        total = total + z_in[step]
-    mine[own_z] = total
+        rows = pl.ds(at_x * depth_x + z_peers[step] * depth_z, depth_z)
+        return remote(mine.at[rows], z_in.at[step], z_send.at[step], z_recv.at[step], z_ids[step])
 
     h_copy = remote(mine.at[own_z], z_in.at[grid_z - 1], h_send, h_recv, h_id)
-    h_copy.start()
-    for way in range(2):
-        advance(way, 4)
-    h_copy.wait()
-    probe_ref[own_z] = mine[own_z] + z_in[grid_z - 1]
 
     def z_back(step, owner):
         rows = pl.ds(at_x * depth_x + owner * depth_z, depth_z)
         return remote(probe_ref.at[rows], probe_ref.at[rows], zg_send.at[step], zg_recv.at[step], z_ids[step])
 
-    for step in range(grid_z - 1):
-        z_back(step, at_z).start()
-    for step in range(grid_z - 1):
-        z_back(step, at_z).wait_send()
-        sender = lax.rem(at_z + grid_z - step - 1, grid_z)
-        z_back(step, sender).wait_recv()
-
     def x_back(step, owner):
         rows = pl.ds(owner * depth_x, depth_x)
         return remote(probe_ref.at[rows], probe_ref.at[rows], xg_send.at[step], xg_recv.at[step], x_ids[step])
 
-    for step in range(grid_x - 1):
-        x_back(step, at_x).start()
-
-    for chip_at in range(CHIPS):
-        @pl.when(chip == chip_at)
+    def after_x():
+        for step in range(grid_x - 1):
+            x_copy(step).wait()
+        total = mine[own_x]
+        for step in range(grid_x - 1):
+            total = total + x_in[step]
+        mine[own_x] = total
+        for step in range(grid_z - 1):
+            z_copy(step).start()
+
+    def after_z():
+        for step in range(grid_z - 1):
+            z_copy(step).wait()
+        total = mine[own_z]
+        for step in range(grid_z - 1):
+            total = total + z_in[step]
+        mine[own_z] = total
+        h_copy.start()
+
+    def after_h():
+        h_copy.wait()
+        probe_ref[own_z] = mine[own_z] + z_in[grid_z - 1]
+        for step in range(grid_z - 1):
+            z_back(step, at_z).start()
+
+    def after_z_back():
+        for step in range(grid_z - 1):
+            z_back(step, at_z).wait_send()
+            z_back(step, lax.rem(at_z + grid_z - step - 1, grid_z)).wait_recv()
+        for step in range(grid_x - 1):
+            x_back(step, at_x).start()
+
+    for here in range(CHIPS):
+        @pl.when(chip == here)
         def _():
-            result = pair_buf[:, chip_at]
-            for way in range(2):
-                copy, out, arrived, rank, blocks = chains[way]
-                here = chip_at if way == 0 else CHIPS - 1 - chip_at
-                if here == 0:
-                    copy(0).wait_recv()
-                    result = result + arrived[0]
+            ready = set()
+
+            def part(block, half):
+                if block not in ready:
+                    ready.add(block)
+                    pair_copy(block).wait()
+                return pair_buf[half, block] + acc_ref[half, 2 * block + core]
+
+            events = [(8.0, 2, after_x), (13.0, 3, after_z), (16.0, 4, after_h), (20.0, 5, after_z_back)]
+            sums = {}
+
+            def arrive(way, rank, item):
+                chain_copy(way, item).wait_recv()
+                block, half = chain_blocks(way)[item // 2], item % 2
+                if rank == CHIPS - 1 and item >= 4 or item >= 4 and stays(item) == rank or rank == 0 and item // 2 == 1:
+                    sums.setdefault(half, []).append(chain_in[way, item])
+                elif rank == 0:
+                    own = part(chain_blocks(way)[4], half)
+                    send(way, 8 + half, own + chain_in[way, item])
                 else:
-                    copy(5 - here).wait_recv()
-                    result = result + arrived[5 - here]
-            object_ref[...] = result
-
-    for way in range(2):
-        copy, out, arrived, rank, blocks = chains[way]
-        for item in range(5):
-            if item < 2:
-                copy(item).wait_send()
-            else:
-                @pl.when(rank < 5 - item)
-                def _():
-                    copy(item).wait_send()
+                    send(way, item, part(block, half) + chain_in[way, item])
+
+            def send(way, item, value):
+                chain_out[way, item] = value
+                chain_copy(way, item).start()
+
+            for way, rank in ((0, here), (1, CHIPS - 1 - here)):
+                for item, time in timetable(rank).items():
+                    events.append((time, way, functools.partial(arrive, way, rank, item)))
+            for item in range(8):
+                for way, rank in ((0, here), (1, CHIPS - 1 - here)):
+                    if rank == 0:
+                        send(way, item, part(chain_blocks(way)[item // 2], item % 2))
+            for _, _, action in sorted(events, key=lambda event: event[:2]):
+                action()
+            for half in range(2):
+                result = part(here, half)
+                for term in sums[half]:
+                    result = result + term
+                object_ref[half] = result
+            for way, rank in ((0, here), (1, CHIPS - 1 - here)):
+                for item in range(10):
+                    if item < 4 or rank < stays(item):
+                        chain_copy(way, item).wait_send()
 
     for step in range(grid_x - 1):
         x_back(step, at_x).wait_send()
-        sender = lax.rem(at_x + grid_x - step - 1, grid_x)
-        x_back(step, sender).wait_recv()
+        x_back(step, lax.rem(at_x + grid_x - step - 1, grid_x)).wait_recv()
+
+
+def chain_blocks(way):
+    return ((5, 4, 3, 2, 1), (6, 7, 0, 1, 2))[way]
+
+
+def stays(item):
+    return 5 - item // 2
+
+
+def timetable(rank, step=2.05):
+    spill = {}
+    for _ in range(2):
+        ready = [{item: 0.0 for item in range(8)}]
+        if spill:
+            ready[0].update({8 + half: spill[half] for half in range(2)})
+        for at in range(CHIPS):
+            clock, arrivals = 0.0, {}
+            for item in range(10):
+                if item in ready[at] and (item < 4 or at < stays(item)):
+                    clock = max(clock, ready[at][item]) + step
+                    arrivals[item] = clock + LATENCY
+            ready.append(arrivals)
+        spill = ready[CHIPS]
+    return spill if rank == 0 else ready[rank]
 
 
 def gather(tiles, grid_x, grid_z, acc, terms):
@@ -561,16 +554,14 @@
         out_specs=(VMEM, VMEM),
         scratch_shapes=[
             pltpu.VMEM((2, 8, 32, WIDTH), F32),
-            pltpu.VMEM((5,) + block, F32),
-            pltpu.VMEM((5,) + block, F32),
-            pltpu.VMEM((5,) + block, F32),
-            pltpu.VMEM((5,) + block, F32),
+            pltpu.VMEM((2, 10, 32, WIDTH), F32),
+            pltpu.VMEM((2, 10, 32, WIDTH), F32),
             pltpu.VMEM((rows, PATCH), F32),
             pltpu.VMEM((rows, PATCH), F32),
             pltpu.VMEM((max(grid_x - 1, 1), depth_x, PATCH), F32),
             pltpu.VMEM((grid_z, depth_z, PATCH), F32),
             dma((8,)), dma((8,)),
-            dma((5,)), dma((5,)), dma((5,)), dma((5,)),
+            dma((2, 10)), dma((2, 10)),
             dma, dma,
             dma((max(grid_x - 1, 1),)), dma((max(grid_x - 1, 1),)),
             dma((grid_z,)), dma((grid_z,)),

time: 287 us -> 138 us (0.48)
  the two profiles are of different devices: /device:TPU:8 before, /device:TPU:1 now
where the time goes in v2:
time: 138 us
  Pallas kernels  131 us (95%)
  local copies, waits for them, and re-layouts  4.82 us (3%)
    pallas_call x1, Pallas kernels, gather(): pl.pallas_call(functools.partial(gather_kernel, tiles, grid_x, grid_z), o...  52 us
    pallas_call x1, Pallas kernels, halo(): pl.pallas_call(functools.partial(halo_kernel, tiles), out_shape=(jax.Shap...  37.9 us
    pallas_call x1, Pallas kernels, sum_power(): pl.pallas_call(sum_kernel, out_shape=jax.ShapeDtypeStruct((rows, PATCH),...  21.5 us
    pallas_call x1, Pallas kernels, back(): pl.pallas_call(back_kernel, out_shape=(jax.ShapeDtypeStruct((2, 2 * STRIP...  10.6 us
    pallas_call x1, Pallas kernels, forward(): pl.pallas_call(forward_kernel, out_shape=(jax.ShapeDtypeStruct((2, 2, PAT...  9.45 us
    unnamed x3, local copies, waits for them, and re-layouts  4.82 us

profile of v2, /device:TPU:1, one launch (start us, length us, event | category | flops | bytes accessed | tf_op | source)
XLA Modules:
  0.0 137.6 jit_solution(4336511019187589378)
XLA Ops:
  1.3 1.3 copy.11.offsets_ref
  2.6 37.9 %halo.1 = (f32[2,512,768]{2,1,0:T(8,128)}, f32[2,2,256,256]{3,2,1,0:T(8,128)}) custom-call(f32[2,256,768]{2,1,0:T(8,128)} %object_ref.1, f32[1,2,256,256]{3,2,1,0:T(8,128)} %probe_ref.1), custom_call_target="tpu_custom_call" | custom-call | tf_op jit(solution)/shard_map/halo/pallas_call | solution.py:130
  40.5 9.4 %forward.1 = (f32[2,2,256,256]{3,2,1,0:T(8,128)}, f32[2,2,2,256,256]{4,3,2,1,0:T(8,128)}, f32[2,256,256]{2,1,0:T(8,128)}) custom-call(f32[2,512,768]{2,1,0:T(8,128)} %get-tuple-element.11.ext_ref, f32[2,2,256,256]{3,2,1,0:T(8,128)} %get-tuple-element.12.modes_ref, s32[4,2]{1,0:T(4,128)} %copy.11.offsets_ref, bf16[512,1536]{1,0:T(8,128)(2,1)} %constant.8.clone.left_ref, ...), custom_call_target="tpu_custom_call" | custom-call | tf_op jit(solution)/shard_map/forward/pallas_call | solution.py:220
  50.0 21.5 %sum_power.1 = f32[512,256]{1,0:T(8,128)} custom-call(f32[512,256]{1,0:T(8,128)} %bitcast.8), custom_call_target="tpu_custom_call" | custom-call | tf_op jit(solution)/shard_map/sum_power/pallas_call | solution.py:295
  71.5 10.6 %back.1 = (f32[2,512,768]{2,1,0:T(8,128)}, f32[2,2,256,256]{3,2,1,0:T(8,128)}) custom-call(f32[2,256,256]{2,1,0:T(8,128)} %bitcast.6, f32[2,2,2,256,256]{4,3,2,1,0:T(8,128)} %get-tuple-element.14.far_ref, f32[2,2,256,256]{3,2,1,0:T(8,128)} %get-tuple-element.15.windows_ref, f32[2,2,256,256]{3,2,1,0:T(8,128)} %get-tuple-element.12.modes_ref, ...), custom_call_target="tpu_custom_call" | custom-call | tf_op jit(solution)/shard_map/back/pallas_call | solution.py:347
  82.1 52.0 %gather.1 = (f32[2,32,768]{2,1,0:T(8,128)}, f32[512,256]{1,0:T(8,128)}) custom-call(f32[2,16,32,768]{3,2,1,0:T(8,128)} %bitcast.5, f32[2,512,256]{2,1,0:T(8,128)} %bitcast.7), custom_call_target="tpu_custom_call" | custom-call | tf_op jit(solution)/shard_map/gather/pallas_call | solution.py:550
  134.1 1.6 %copy.16 = f32[2,32,768]{2,1,0:T(8,128)} copy(f32[2,32,768]{2,1,0:T(8,128)} %get-tuple-element.22) | data formatting | bytes 393216
  135.7 1.9 %copy.17 = f32[1,2,256,256]{3,2,1,0:T(8,128)} copy(f32[1,2,256,256]{3,2,1,0:T(8,128)} %bitcast.9) | data formatting | bytes 1048576

commit v3 on v0

v3 whole, which is shorter than its diff:
```python
import functools
import math

import jax
import jax.numpy as jnp
import numpy as np
from jax import lax
from jax.experimental import pallas as pl
from jax.experimental.pallas import tpu as pltpu
from jax.sharding import PartitionSpec as P

MESH = pl.DeviceIdType.MESH
F32 = jnp.float32
BF16 = jnp.bfloat16
VMEM = pl.BlockSpec(memory_space=pltpu.VMEM)
SMEM = pl.BlockSpec(memory_space=pltpu.SMEM)
ANY = pl.BlockSpec(memory_space=pl.ANY)
LIMIT = 56 * 1024 * 1024
PATCH = 256
STRIP = 256
WIDTH = 768
CAP = 4
CHIPS = 4
PAIR = 2

HALO_CUTS = 8
SUM_CUTS = 8
LATENCY = 2.3


def split(value):
    high = value.astype(BF16)
    return high, (value - high.astype(F32)).astype(BF16)


def dft_tables():
    index = np.arange(PATCH)
    angle = 2.0 * math.pi * ((index[:, None] * index[None, :]) % PATCH) / PATCH
    cos, sine = np.cos(angle) / math.sqrt(PATCH), -np.sin(angle) / math.sqrt(PATCH)

    def parts(block):
        high = block.astype(jnp.bfloat16)
        low = (block - high.astype(np.float64)).astype(jnp.bfloat16)
        return high, low

    high, low = parts(np.block([[cos, -sine], [sine, cos]]))
    left = np.concatenate([high, high, low], axis=1)
    high, low = parts(np.block([[cos, sine], [-sine, cos]]))
    right = np.concatenate([high, high, low], axis=0)
    return left, right


def transform(real, imag, left, right):
    high, low = split(jnp.concatenate([real, imag], axis=0))
    mid = jnp.dot(left[...], jnp.concatenate([high, low, high], axis=0), preferred_element_type=F32)
    high, low = split(jnp.concatenate([mid[:PATCH], mid[PATCH:]], axis=1))
    out = jnp.dot(jnp.concatenate([high, low, high], axis=1), right[...], preferred_element_type=F32)
    return out[:, :PATCH], out[:, PATCH:]


def selector(shape, source, target, offset):
    index = lax.broadcasted_iota(jnp.int32, shape, source) - lax.broadcasted_iota(jnp.int32, shape, target)
    return jnp.where(index == offset, 1.0, 0.0).astype(BF16)


def select(left, right):
    return jnp.dot(left, right, preferred_element_type=F32)


def remote(source, target, send_sem, recv_sem, device):
    return pltpu.make_async_remote_copy(
        src_ref=source, dst_ref=target, send_sem=send_sem, recv_sem=recv_sem, device_id=device, device_id_type=MESH
    )


def by_chip(chip, action):
    for here in range(CHIPS):
        pl.when(chip == here)(functools.partial(action, here))


def ranks(here):
    return ((0, here), (1, CHIPS - 1 - here))


def kernel(tiles, grid_x, grid_z, object_hbm, probe_hbm, measured_ref, offsets_ref, counts_ref, left_hbm, right_hbm,
           object_ref, probe_ref,
           ext, modes, left, right, windows, far, power, staged, arrived, cut_columns,
           cut_rows, put_columns, put_rows, strips, moved, acc, terms, pair_buf, chain_out,
           chain_in, probe_buf, mine, x_in, z_in, local_sem, swap_send, swap_recv, halo_send, halo_recv, cross_send,
           cross_recv, sum_send, sum_recv, pair_send, pair_recv, chain_send, chain_recv, probe_send, probe_recv, x_send,
           x_recv, z_send, z_recv, h_send, h_recv, zg_send, zg_recv, xg_send, xg_recv):
    tile, mode = lax.axis_index("tile"), lax.axis_index("mode")
    chip, core = mode // 2, mode % 2
    high, plane = tile % 2, tile // 2
    at_z, at_x = plane % grid_z, plane // grid_z
    after, before = lax.rem(tile + 1, tiles), lax.rem(tile + tiles - 1, tiles)
    sibling = (tile, mode + 1 - 2 * core)
    above = jnp.where(chip < 3, mode + 2, core)
    below = jnp.where(chip > 0, mode - 2, core + 6)
    next_above, last_above = (jnp.where(chip < 3, tile, after), above), (jnp.where(chip < 3, tile, before), above)
    next_below, last_below = (jnp.where(chip > 0, tile, after), below), (jnp.where(chip > 0, tile, before), below)

    def at(x, z, h):
        return ((x * grid_z + z) * 2 + h, mode)

    x_peers = [lax.rem(at_x + step, grid_x) for step in range(1, grid_x)]
    z_peers = [lax.rem(at_z + step, grid_z) for step in range(1, grid_z)]
    x_ids = [at(peer, at_z, high) for peer in x_peers]
    z_ids = [at(at_x, peer, high) for peer in z_peers]
    h_id = at(at_x, at_z, 1 - high)

    own_copy = pltpu.make_async_copy(object_hbm, ext.at[:, pl.ds(0, STRIP)], local_sem.at[0])
    probe_copy = pltpu.make_async_copy(probe_hbm.at[0], modes.at[core], local_sem.at[1])
    left_copy = pltpu.make_async_copy(left_hbm, left, local_sem.at[2])
    right_copy = pltpu.make_async_copy(right_hbm, right, local_sem.at[3])
    for copy in (own_copy, probe_copy, left_copy, right_copy):
        copy.start()
    barrier = pltpu.get_barrier_semaphore()
    friends = [next_above, last_above, next_below, last_below, sibling, h_id] + x_ids + z_ids
    for device in friends:
        pl.semaphore_signal(barrier, inc=1, device_id=device, device_id_type=MESH)
    pl.semaphore_wait(barrier, len(friends))

    swap = remote(probe_hbm.at[0], modes.at[core], swap_send, swap_recv, sibling)
    depth = STRIP // 4 // HALO_CUTS
    down_first = (last_below, last_above)

    def halo_rows(way, cut, owner):
        return (2 * way + owner) * (STRIP // 4) + cut * depth

    def halo_copy(way, cut, base):
        row = halo_rows(way, cut, core)
        return remote(
            ext.at[:, pl.ds(base + row, depth)],
            ext.at[:, pl.ds(STRIP + row, depth)],
            halo_send.at[way, cut],
            halo_recv.at[way, cut],
            down_first[way],
        )

    def cross_copy(way, cut, owner):
        block = ext.at[:, pl.ds(STRIP + halo_rows(way, cut, owner), depth)]
        return remote(block, block, cross_send.at[way, cut], cross_recv.at[way, cut], sibling)

    own_copy.wait()
    for way, last in ((0, 0), (1, 3)):
        @pl.when(chip == last)
        def _():
            for cut in range(HALO_CUTS):
                halo_copy(way, cut, 0).start()
    swap.start()
    for slot in range(2):
        row, column = offsets_ref[2 * core + slot, 0], offsets_ref[2 * core + slot, 1]
        own = pl.ds(slot * PATCH, PATCH)
        cut_columns[:, own] = selector((WIDTH, PATCH), 0, 1, column)
        put_columns[slot] = selector((PATCH, WIDTH), 1, 0, column)
        for copy in range(2):
            cut_rows[slot, :, pl.ds(copy * 2 * STRIP, 2 * STRIP)] = selector((PATCH, 2 * STRIP), 1, 0, row)
            put_rows[:, pl.ds((2 * copy + slot) * PATCH, PATCH)] = selector((2 * STRIP, PATCH), 0, 1, row)

    def cut_strip(first):
        for part in range(2):
            for index, value in enumerate(split(ext[part, pl.ds(first, STRIP)])):
                strips[part, pl.ds(index * 2 * STRIP + first, STRIP)] = select(value, cut_columns[...]).astype(BF16)

    cut_strip(0)

    def halo_events(here):
        step = 8.0 / HALO_CUTS
        events = []
        for way, rank in ((0, CHIPS - 1 - here), (1, here)):
            for cut in range(HALO_CUTS):
                events.append(((rank + 1) * (step + LATENCY) + cut * step, way, cut, rank < CHIPS - 1))
        for _, way, cut, forwards in sorted(events):
            halo_copy(way, cut, 0).wait_recv()
            if forwards:
                halo_copy(way, cut, STRIP).start()
            cross_copy(way, cut, core).start()

    by_chip(chip, halo_events)
    probe_copy.wait()
    swap.wait_recv()
    left_copy.wait()
    right_copy.wait()
    for cut in range(HALO_CUTS):
        for way in range(2):
            cross_copy(way, cut, 1 - core).wait_recv()

    sum_depth = PATCH // SUM_CUTS

    def sum_copy(way, slot, cut, source):
        rows = pl.ds(cut * sum_depth, sum_depth)
        item = slot * SUM_CUTS + cut
        return remote(
            source.at[slot, rows],
            arrived.at[way, slot, rows],
            sum_send.at[way, item],
            sum_recv.at[way, item],
            ((tile, mode + 2), (tile, mode - 2))[way],
        )

    def forward(slot):
        window = []
        for part in range(2):
            block = select(cut_rows[slot], strips[part, :, pl.ds(slot * PATCH, PATCH)])
            windows[slot, part] = block
            window.append(block)
        for pair in range(PAIR):
            mode_real, mode_imag = modes[pair, 0], modes[pair, 1]
            far_real, far_imag = transform(
                mode_real * window[0] - mode_imag * window[1],
                mode_real * window[1] + mode_imag * window[0],
                left,
                right,
            )
            far[slot, pair, 0] = far_real
            far[slot, pair, 1] = far_imag
            if pair == 0:
                power[slot] = far_real * far_real + far_imag * far_imag
            else:
                power[slot] += far_real * far_real + far_imag * far_imag

    def first_sums(slot):
        for way, first in ((0, 0), (1, 3)):
            @pl.when(chip == first)
            def _():
                for cut in range(SUM_CUTS):
                    sum_copy(way, slot, cut, power).start()

    cut_strip(STRIP)
    for slot in range(2):
        forward(slot)
        first_sums(slot)

    def sum_events(here):
        step = 5.3 / SUM_CUTS
        events = []
        for way, rank in ranks(here):
            if rank > 0:
                for slot in range(2):
                    for cut in range(SUM_CUTS):
                        time = rank * (step + LATENCY) + (slot * SUM_CUTS + cut) * step
                        events.append((time, way, slot, cut, rank < CHIPS - 1))
        for _, way, slot, cut, forwards in sorted(events):
            sum_copy(way, slot, cut, power).wait_recv()
            if forwards:
                rows = pl.ds(cut * sum_depth, sum_depth)
                staged[way, slot, rows] = power[slot, rows] + arrived[way, slot, rows]
                sum_copy(way, slot, cut, staged.at[way]).start()

    by_chip(chip, sum_events)

    def intensity(slot):
        lower = jnp.where(chip > 0, arrived[0, slot], 0.0)
        upper = jnp.where(chip < 3, arrived[1, slot], 0.0)
        return power[slot] + (lower + upper)

    def backward(slot):
        index = 2 * core + slot
        amplitude = jnp.sqrt(measured_ref[index].astype(F32))
        live = (index < counts_ref[0]).astype(F32)
        scaling = live * (1.0 - amplitude / jnp.sqrt(jnp.maximum(intensity(slot), 1.0)))
        win_real, win_imag = windows[slot, 0], windows[slot, 1]
        sums = None
        for pair in range(PAIR):
            back_real, minus_imag = transform(
                scaling * far[slot, pair, 0], -(scaling * far[slot, pair, 1]), left, right
            )
            mode_real, mode_imag = modes[pair, 0], modes[pair, 1]
            grads = (
                mode_real * back_real - mode_imag * minus_imag,
                -(mode_real * minus_imag + mode_imag * back_real),
            )
            sums = grads if sums is None else (sums[0] + grads[0], sums[1] + grads[1])
            probe_real = win_real * back_real - win_imag * minus_imag
            probe_imag = -(win_real * minus_imag + win_imag * back_real)
            if slot == 0:
                terms[pair, pl.ds(0, PATCH)] = probe_real
                terms[pair, pl.ds(PATCH, PATCH)] = probe_imag
            else:
                terms[pair, pl.ds(0, PATCH)] += probe_real
                terms[pair, pl.ds(PATCH, PATCH)] += probe_imag
        for part, term in enumerate(sums):
            for copy, value in enumerate(split(term)):
                rows = pl.ds((2 * copy + slot) * PATCH, PATCH)
                moved[part, rows] = select(value, put_columns[slot]).astype(BF16)

    for slot in range(2):
        backward(slot)

    probe_pair = remote(terms.at[1 - core], probe_buf, probe_send, probe_recv, sibling)
    probe_pair.start()

    def pair_copy(block):
        return remote(
            acc.at[:, 2 * block + 1 - core], pair_buf.at[:, block], pair_send.at[block], pair_recv.at[block], sibling
        )

    for first, blocks in ((STRIP, (5, 6, 4, 7)), (0, (3, 0, 2, 1))):
        for half in range(2):
            total = select(put_rows[pl.ds(first, STRIP)], moved[half])
            for index in range(8):
                acc[half, first // 32 + index] = total[32 * index : 32 * index + 32]
        for block in blocks:
            pair_copy(block).start()

    depth_x = 2 * PATCH // grid_x
    depth_z = depth_x // grid_z
    probe_pair.wait_recv()
    mine[...] = probe_buf[...] + terms[core]

    def x_copy(step):
        peer = x_peers[step]
        return remote(
            mine.at[pl.ds(peer * depth_x, depth_x)], x_in.at[step], x_send.at[step], x_recv.at[step], x_ids[step]
        )

    for step in range(grid_x - 1):
        x_copy(step).start()

    def chain_copy(way, item):
        return remote(
            chain_out.at[way, item], chain_in.at[way, item], chain_send.at[way, item], chain_recv.at[way, item],
            (next_above, next_below)[way],
        )

    own_x = pl.ds(at_x * depth_x, depth_x)
    own_z = pl.ds(at_x * depth_x + at_z * depth_z, depth_z)

    def z_copy(step):
        rows = pl.ds(at_x * depth_x + z_peers[step] * depth_z, depth_z)
        return remote(mine.at[rows], z_in.at[step], z_send.at[step], z_recv.at[step], z_ids[step])

    h_copy = remote(mine.at[own_z], z_in.at[grid_z - 1], h_send, h_recv, h_id)

    def z_back(step, owner):
        rows = pl.ds(at_x * depth_x + owner * depth_z, depth_z)
        return remote(probe_ref.at[rows], probe_ref.at[rows], zg_send.at[step], zg_recv.at[step], z_ids[step])

    def x_back(step, owner):
        rows = pl.ds(owner * depth_x, depth_x)
        return remote(probe_ref.at[rows], probe_ref.at[rows], xg_send.at[step], xg_recv.at[step], x_ids[step])

    def after_x():
        for step in range(grid_x - 1):
            x_copy(step).wait()
        total = mine[own_x]
        for step in range(grid_x - 1):
            total = total + x_in[step]
        mine[own_x] = total
        for step in range(grid_z - 1):
            z_copy(step).start()

    def after_z():
        for step in range(grid_z - 1):
            z_copy(step).wait()
        total = mine[own_z]
        for step in range(grid_z - 1):
            total = total + z_in[step]
        mine[own_z] = total
        h_copy.start()

    def after_h():
        h_copy.wait()
        probe_ref[own_z] = mine[own_z] + z_in[grid_z - 1]
        for step in range(grid_z - 1):
            z_back(step, at_z).start()

    def after_z_back():
        for step in range(grid_z - 1):
            z_back(step, at_z).wait_send()
            z_back(step, lax.rem(at_z + grid_z - step - 1, grid_z)).wait_recv()
        for step in range(grid_x - 1):
            x_back(step, at_x).start()

    def chain_events(here):
        ready = set()

        def part(block, half):
            if block not in ready:
                ready.add(block)
                pair_copy(block).wait_recv()
            return pair_buf[half, block] + acc[half, 2 * block + core]

        def send(way, item, value):
            chain_out[way, item] = value
            chain_copy(way, item).start()

        sums = {}

        def arrive(way, rank, item):
            chain_copy(way, item).wait_recv()
            blocks, half = chain_blocks(way), item % 2
            if item >= 4 and stays(item) == rank or rank == 0 and item // 2 == 1:
                sums.setdefault(half, []).append(chain_in[way, item])
            elif rank == 0:
                send(way, 8 + half, part(blocks[4], half) + chain_in[way, item])
            else:
                send(way, item, part(blocks[item // 2], half) + chain_in[way, item])

        for item in range(8):
            for way, rank in ranks(here):
                if rank == 0:
                    send(way, item, part(chain_blocks(way)[item // 2], item % 2))
        events = [(8.0, 2, after_x), (13.0, 3, after_z), (16.0, 4, after_h), (20.0, 5, after_z_back)]
        for way, rank in ranks(here):
            for item, time in timetable(rank).items():
                events.append((time, way, functools.partial(arrive, way, rank, item)))
        for _, _, action in sorted(events, key=lambda event: event[:2]):
            action()
        for half in range(2):
            result = part(here, half)
            for term in sums[half]:
                result = result + term
            object_ref[half] = result

    by_chip(chip, chain_events)
    for step in range(grid_x - 1):
        x_back(step, lax.rem(at_x + grid_x - step - 1, grid_x)).wait_recv()

    def sends(here):
        for way, rank in ranks(here):
            for item in range(10):
                if item < 4 or rank < stays(item):
                    chain_copy(way, item).wait_send()
            if rank < CHIPS - 1:
                for slot in range(2):
                    for cut in range(SUM_CUTS):
                        sum_copy(way, slot, cut, power).wait_send()

    by_chip(chip, sends)
    swap.wait_send()
    probe_pair.wait_send()
    for cut in range(HALO_CUTS):
        for way in range(2):
            halo_copy(way, cut, 0).wait_send()
            cross_copy(way, cut, core).wait_send()
    for block in range(8):
        pair_copy(block).wait_send()
    for step in range(grid_x - 1):
        x_back(step, at_x).wait_send()


def chain_blocks(way):
    return ((5, 4, 3, 2, 1), (6, 7, 0, 1, 2))[way]


def stays(item):
    return 5 - item // 2


def timetable(rank, step=2.05):
    spill = {}
    for _ in range(2):
        ready = [{item: 0.0 for item in range(8)}]
        if spill:
            ready[0].update({8 + half: spill[half] for half in range(2)})
        for at in range(CHIPS):
            clock, arrivals = 0.0, {}
            for item in range(10):
                if item in ready[at] and (item < 4 or at < stays(item)):
                    clock = max(clock, ready[at][item]) + step
                    arrivals[item] = clock + LATENCY
            ready.append(arrivals)
        spill = ready[CHIPS]
    return spill if rank == 0 else ready[rank]


def solution(mesh):
    tiles = mesh.shape["tile"]
    grid_x = 4 if tiles == 64 else 2
    grid_z = tiles // 2 // grid_x
    left, right = dft_tables()
    rows = 2 * PATCH
    depth_x = rows // grid_x
    depth_z = depth_x // grid_z
    block = (2, 32, WIDTH)
    dma = pltpu.SemaphoreType.DMA

    def body(object_field, probe_modes, measured, offsets, counts):
        object_rows, probe = pl.pallas_call(
            functools.partial(kernel, tiles, grid_x, grid_z),
            out_shape=(jax.ShapeDtypeStruct(block, F32), jax.ShapeDtypeStruct((rows, PATCH), F32)),
            in_specs=[ANY, ANY, VMEM, SMEM, SMEM, ANY, ANY],
            out_specs=(VMEM, VMEM),
            scratch_shapes=[
                pltpu.VMEM((2, 2 * STRIP, WIDTH), F32),
                pltpu.VMEM((PAIR, 2, PATCH, PATCH), F32),
                pltpu.VMEM(left.shape, BF16),
                pltpu.VMEM(right.shape, BF16),
                pltpu.VMEM((2, 2, PATCH, PATCH), F32),
                pltpu.VMEM((2, PAIR, 2, PATCH, PATCH), F32),
                pltpu.VMEM((2, PATCH, PATCH), F32),
                pltpu.VMEM((2, 2, PATCH, PATCH), F32),
                pltpu.VMEM((2, 2, PATCH, PATCH), F32),
                pltpu.VMEM((WIDTH, 2 * PATCH), BF16),
                pltpu.VMEM((2, PATCH, 4 * STRIP), BF16),
                pltpu.VMEM((2, PATCH, WIDTH), BF16),
                pltpu.VMEM((2 * STRIP, 4 * PATCH), BF16),
                pltpu.VMEM((2, 4 * STRIP, 2 * PATCH), BF16),
                pltpu.VMEM((2, 4 * PATCH, WIDTH), BF16),
                pltpu.VMEM((2, 16, 32, WIDTH), F32),
                pltpu.VMEM((PAIR, rows, PATCH), F32),
                pltpu.VMEM((2, 8, 32, WIDTH), F32),
                pltpu.VMEM((2, 10, 32, WIDTH), F32),
                pltpu.VMEM((2, 10, 32, WIDTH), F32),
                pltpu.VMEM((rows, PATCH), F32),
                pltpu.VMEM((rows, PATCH), F32),
                pltpu.VMEM((grid_x - 1, depth_x, PATCH), F32),
                pltpu.VMEM((grid_z, depth_z, PATCH), F32),
                dma((4,)),
                dma, dma,
                dma((2, HALO_CUTS)), dma((2, HALO_CUTS)),
                dma((2, HALO_CUTS)), dma((2, HALO_CUTS)),
                dma((2, 2 * SUM_CUTS)), dma((2, 2 * SUM_CUTS)),
                dma((8,)), dma((8,)),
                dma((2, 10)), dma((2, 10)),
                dma, dma,
                dma((grid_x - 1,)), dma((grid_x - 1,)),
                dma((grid_z,)), dma((grid_z,)),
                dma, dma,
                dma((grid_z,)), dma((grid_z,)),
                dma((grid_x - 1,)), dma((grid_x - 1,)),
            ],
            compiler_params=pltpu.CompilerParams(collective_id=0, has_side_effects=True, vmem_limit_bytes=LIMIT),
            name="ptychography",
        )(object_field, probe_modes, measured, offsets, counts, jnp.asarray(left), jnp.asarray(right))
        return object_rows, probe.reshape(1, 2, PATCH, PATCH)

    return jax.shard_map(
        body,
        mesh=mesh,
        in_specs=(
            P(None, "tile", None),
            P("mode", None, None, None),
            P("tile", None, None),
            P("tile", None),
            P("tile"),
        ),
        out_specs=(P(None, ("tile", "mode"), None), P("mode", None, None, None)),
        check_vma=False,
    )
```

time: 1210 us -> 117 us (0.10); the launches traced: 1200 us -> 116 us
  waiting for transfers between devices: 1030 us -> 0 us
  Pallas kernels: 0 us -> 110 us
  matrix products: 50.8 us -> 0 us
  local copies, waits for them, and re-layouts: 45.2 us -> 4.82 us
  between operations: 29.9 us -> 1.29 us
  starting transfers between devices: 28.3 us -> 0 us
  other arithmetic: 12.4 us -> 0 us
    psum x2 -> x0, waiting for transfers between devices: 811 us -> none  [the longest x1 750 us: body(): probe_total = lax.psum(jnp.stack([probe_real, probe_imag]), 'tile')]
    ppermute x2 -> x0, waiting for transfers between devices: 137 us -> none  [from_behind(): return lax.ppermute(value, axis, pairs)]
    pallas_call x0 -> x1, Pallas kernels: none -> 110 us  [body(): pl.pallas_call(functools.partial(kernel, tiles, grid_x, grid_z), out_shap...]
    reduce_scatter x1 -> x0, waiting for transfers between devices: 80.8 us -> none  [body(): lax.psum_scatter(own_rows + arriving, 'mode', scatter_dimension=1, tiled=...]
    dot_general x16 -> x0, matrix products: 50.8 us -> none  [the longest x8 26.4 us: left_apply(): return jnp.einsum('jk,skl->sjl', table, stack, precision=HIGHEST)]
    ppermute x2 -> x0, starting transfers between devices: 27.9 us -> none  [from_behind(): return lax.ppermute(value, axis, pairs)]
    dynamic_update_slice x4 -> x0, local copies, waits for them, and re-layouts: 22.9 us -> none  [body(): lax.dynamic_update_slice(accumulated, current + object_terms[slot_index],...]
    gather x12 -> x0, local copies, waits for them, and re-layouts: 13.1 us -> none
  transfers between devices with their start and end apart: 5 -> 0, of which waited for: 5 -> 0; matrix products, arithmetic and copies ran while one was open for 1% -> 0% of each run, Pallas kernels for 0% -> 0%
where the time goes in v3:
time: 117 us; the launch traced here: 116 us
  Pallas kernels  110 us (94%)
  local copies, waits for them, and re-layouts  4.82 us (4%)
  between operations  1.29 us (1%)
    pallas_call x1, Pallas kernels, body(): pl.pallas_call(functools.partial(kernel, tiles, grid_x, grid_z), out_shap...  110 us
    unnamed x3, local copies, waits for them, and re-layouts  4.82 us

profile of v3, /device:TPU:1, one launch (start us, length us, event | category | flops | bytes accessed | tf_op | source)
XLA Modules:
  0.0 116.1 jit_solution(4253542159057452854)
XLA Ops:
  1.3 1.3 %copy.9.offsets_ref = s32[4,2]{1,0:T(4,128)} copy(s32[4,2]{0,1:T(2,128)} %param.10) | data formatting | bytes 64 | tf_op args[3]
  2.6 110.0 %ptychography.1 = (f32[2,32,768]{2,1,0:T(8,128)}, f32[512,256]{1,0:T(8,128)}) custom-call(f32[2,256,768]{2,1,0:T(8,128)} %object_hbm.1, f32[1,2,256,256]{3,2,1,0:T(8,128)} %probe_hbm.1, bf16[4,256,256]{2,1,0:T(8,128)(2,1)} %measured_ref.1, s32[4,2]{1,0:T(4,128)} %copy.9.offsets_ref, s32[1]{0:T(128)S(6)} %copy.12.counts_ref, ...), custom_call_target="tpu_custom_call" | custom-call | tf_op jit(solution)/shard_map/ptychography/pallas_call | solution.py:481
  112.7 1.6 %copy.13 = f32[2,32,768]{2,1,0:T(8,128)} copy(f32[2,32,768]{2,1,0:T(8,128)} %get-tuple-element.8) | data formatting | bytes 393216
  114.3 1.9 %copy.14 = f32[1,2,256,256]{3,2,1,0:T(8,128)} copy(f32[1,2,256,256]{3,2,1,0:T(8,128)} %bitcast.1) | data formatting | bytes 1048576

commit v4 on v3

--- a/solution.py
+++ b/solution.py
@@ -86,9 +86,9 @@
            object_ref, probe_ref,
            ext, modes, left, right, windows, far, power, staged, arrived, cut_columns,
            cut_rows, put_columns, put_rows, strips, moved, acc, terms, pair_buf, chain_out,
-           chain_in, probe_buf, mine, x_in, z_in, local_sem, swap_send, swap_recv, halo_send, halo_recv, cross_send,
-           cross_recv, sum_send, sum_recv, pair_send, pair_recv, chain_send, chain_recv, probe_send, probe_recv, x_send,
-           x_recv, z_send, z_recv, h_send, h_recv, zg_send, zg_recv, xg_send, xg_recv):
+           chain_in, probe_buf, mine, result, px_in, qz_in, pz_in, qx_in, local_sem, swap_send, swap_recv, halo_send, halo_recv, cross_send,
+           cross_recv, sum_send, sum_recv, pair_send, pair_recv, chain_send, chain_recv, probe_send, probe_recv, px_send,
+           px_recv, qz_send, qz_recv, pz_send, pz_recv, qx_send, qx_recv):
     tile, mode = lax.axis_index("tile"), lax.axis_index("mode")
     chip, core = mode // 2, mode % 2
     high, plane = tile % 2, tile // 2
@@ -103,12 +103,6 @@
     def at(x, z, h):
         return ((x * grid_z + z) * 2 + h, mode)
 
-    x_peers = [lax.rem(at_x + step, grid_x) for step in range(1, grid_x)]
-    z_peers = [lax.rem(at_z + step, grid_z) for step in range(1, grid_z)]
-    x_ids = [at(peer, at_z, high) for peer in x_peers]
-    z_ids = [at(at_x, peer, high) for peer in z_peers]
-    h_id = at(at_x, at_z, 1 - high)
-
     own_copy = pltpu.make_async_copy(object_hbm, ext.at[:, pl.ds(0, STRIP)], local_sem.at[0])
     probe_copy = pltpu.make_async_copy(probe_hbm.at[0], modes.at[core], local_sem.at[1])
     left_copy = pltpu.make_async_copy(left_hbm, left, local_sem.at[2])
@@ -116,7 +110,11 @@
     for copy in (own_copy, probe_copy, left_copy, right_copy):
         copy.start()
     barrier = pltpu.get_barrier_semaphore()
-    friends = [next_above, last_above, next_below, last_below, sibling, h_id] + x_ids + z_ids
+    friends = [next_above, last_above, next_below, last_below, sibling]
+    friends += [at(lax.rem(at_x + step, grid_x), at_z, high) for step in range(1, grid_x)]
+    friends += [at(lax.rem(at_x + step, grid_x), at_z, 1 - high) for step in range(grid_x)]
+    friends += [at(at_x, lax.rem(at_z + step, grid_z), high) for step in range(1, grid_z)]
+    friends += [at(at_x, lax.rem(at_z + step, grid_z), 1 - high) for step in range(1, grid_z)]
     for device in friends:
         pl.semaphore_signal(barrier, inc=1, device_id=device, device_id_type=MESH)
     pl.semaphore_wait(barrier, len(friends))
@@ -140,7 +138,7 @@
 
     def cross_copy(way, cut, owner):
         block = ext.at[:, pl.ds(STRIP + halo_rows(way, cut, owner), depth)]
-        return remote(block, block, cross_send.at[way, cut], cross_recv.at[way, cut], sibling)
+        return remote(block, block, cross_send, cross_recv, sibling)
 
     own_copy.wait()
     for way, last in ((0, 0), (1, 3)):
@@ -150,7 +148,7 @@
                 halo_copy(way, cut, 0).start()
     swap.start()
     for slot in range(2):
-        row, column = offsets_ref[2 * core + slot, 0], offsets_ref[2 * core + slot, 1]
+        row, column = offsets_ref[0, 2 * core + slot], offsets_ref[1, 2 * core + slot]
         own = pl.ds(slot * PATCH, PATCH)
         cut_columns[:, own] = selector((WIDTH, PATCH), 0, 1, column)
         put_columns[slot] = selector((PATCH, WIDTH), 1, 0, column)
@@ -158,12 +156,9 @@
             cut_rows[slot, :, pl.ds(copy * 2 * STRIP, 2 * STRIP)] = selector((PATCH, 2 * STRIP), 1, 0, row)
             put_rows[:, pl.ds((2 * copy + slot) * PATCH, PATCH)] = selector((2 * STRIP, PATCH), 0, 1, row)
 
-    def cut_strip(first):
-        for part in range(2):
-            for index, value in enumerate(split(ext[part, pl.ds(first, STRIP)])):
-                strips[part, pl.ds(index * 2 * STRIP + first, STRIP)] = select(value, cut_columns[...]).astype(BF16)
-
-    cut_strip(0)
+    def cut_strip(part, first, depth):
+        for index, value in enumerate(split(ext[part, pl.ds(first, depth)])):
+            strips[part, pl.ds(index * 2 * STRIP + first, depth)] = select(value, cut_columns[...]).astype(BF16)
 
     def halo_events(here):
         step = 8.0 / HALO_CUTS
@@ -171,20 +166,23 @@
         for way, rank in ((0, CHIPS - 1 - here), (1, here)):
             for cut in range(HALO_CUTS):
                 events.append(((rank + 1) * (step + LATENCY) + cut * step, way, cut, rank < CHIPS - 1))
-        for _, way, cut, forwards in sorted(events):
+        for index, (_, way, cut, forwards) in enumerate(sorted(events)):
             halo_copy(way, cut, 0).wait_recv()
             if forwards:
                 halo_copy(way, cut, STRIP).start()
             cross_copy(way, cut, core).start()
+            if index in (1, 4, 7, 10):
+                piece = (1, 4, 7, 10).index(index)
+                cut_strip(piece // 2, piece % 2 * 128, 128)
 
     by_chip(chip, halo_events)
     probe_copy.wait()
     swap.wait_recv()
     left_copy.wait()
     right_copy.wait()
-    for cut in range(HALO_CUTS):
-        for way in range(2):
-            cross_copy(way, cut, 1 - core).wait_recv()
+    crossed = ext.at[:, pl.ds(STRIP, STRIP // 2)]
+    all_across = remote(crossed, crossed, cross_send, cross_recv, sibling)
+    all_across.wait_recv()
 
     sum_depth = PATCH // SUM_CUTS
 
@@ -227,12 +225,13 @@
                 for cut in range(SUM_CUTS):
                     sum_copy(way, slot, cut, power).start()
 
-    cut_strip(STRIP)
+    for part in range(2):
+        cut_strip(part, STRIP, STRIP)
     for slot in range(2):
         forward(slot)
         first_sums(slot)
 
-    def sum_events(here):
+    def sum_events(late, here):
         step = 5.3 / SUM_CUTS
         events = []
         for way, rank in ranks(here):
@@ -242,13 +241,13 @@
                         time = rank * (step + LATENCY) + (slot * SUM_CUTS + cut) * step
                         events.append((time, way, slot, cut, rank < CHIPS - 1))
         for _, way, slot, cut, forwards in sorted(events):
+            if late != (not forwards and slot == 1):
+                continue
             sum_copy(way, slot, cut, power).wait_recv()
             if forwards:
                 rows = pl.ds(cut * sum_depth, sum_depth)
                 staged[way, slot, rows] = power[slot, rows] + arrived[way, slot, rows]
                 sum_copy(way, slot, cut, staged.at[way]).start()
-
-    by_chip(chip, sum_events)
 
     def intensity(slot):
         lower = jnp.where(chip > 0, arrived[0, slot], 0.0)
@@ -262,7 +261,7 @@
         scaling = live * (1.0 - amplitude / jnp.sqrt(jnp.maximum(intensity(slot), 1.0)))
         win_real, win_imag = windows[slot, 0], windows[slot, 1]
         sums = None
-        for pair in range(PAIR):
+        for pair in (1 - core, core):
             back_real, minus_imag = transform(
                 scaling * far[slot, pair, 0], -(scaling * far[slot, pair, 1]), left, right
             )
@@ -280,23 +279,30 @@
             else:
                 terms[pair, pl.ds(0, PATCH)] += probe_real
                 terms[pair, pl.ds(PATCH, PATCH)] += probe_imag
+                if pair is not core:
+                    probe_pair.start()
         for part, term in enumerate(sums):
             for copy, value in enumerate(split(term)):
                 rows = pl.ds((2 * copy + slot) * PATCH, PATCH)
                 moved[part, rows] = select(value, put_columns[slot]).astype(BF16)
 
-    for slot in range(2):
-        backward(slot)
-
     probe_pair = remote(terms.at[1 - core], probe_buf, probe_send, probe_recv, sibling)
-    probe_pair.start()
+    swap.wait_send()
+    all_across.wait_send()
+    for cut in range(HALO_CUTS):
+        for way in range(2):
+            halo_copy(way, cut, 0).wait_send()
+    by_chip(chip, functools.partial(sum_events, False))
+    backward(0)
+    by_chip(chip, functools.partial(sum_events, True))
+    backward(1)
 
     def pair_copy(block):
         return remote(
             acc.at[:, 2 * block + 1 - core], pair_buf.at[:, block], pair_send.at[block], pair_recv.at[block], sibling
         )
 
-    for first, blocks in ((STRIP, (5, 6, 4, 7)), (0, (3, 0, 2, 1))):
+    def put(first, blocks):
         for half in range(2):
             total = select(put_rows[pl.ds(first, STRIP)], moved[half])
             for index in range(8):
@@ -304,19 +310,97 @@
         for block in blocks:
             pair_copy(block).start()
 
-    depth_x = 2 * PATCH // grid_x
-    depth_z = depth_x // grid_z
+    def group_x(index):
+        return at(index, at_z, high)
+
+    def group_z(index):
+        return at(at_x, index, high)
+
+    def group_zh(index):
+        return at(at_x, index // 2, index % 2)
+
+    def group_xh(index):
+        return at(index // 2, at_z, index % 2)
+
+    half_tiles = mine.shape[0] // 2
+    x_tiles, z_tiles = half_tiles // grid_x, half_tiles // grid_z
+    outer = (
+        (group_x, grid_x, at_x, 0, x_tiles, px_in, px_send, px_recv),
+        (group_z, grid_z, at_z, half_tiles, z_tiles, qz_in, qz_send, qz_recv),
+    )
+    inner = (
+        (group_zh, 2 * grid_z, 2 * at_z + high, at_x * x_tiles, x_tiles // (2 * grid_z), pz_in, pz_send, pz_recv),
+        (group_xh, 2 * grid_x, 2 * at_x + high, half_tiles + at_z * z_tiles, z_tiles // (2 * grid_x), qx_in, qx_send,
+         qx_recv),
+    )
+
+    def scatter_copy(stage, step):
+        group, count, here, base, depth, inbox, send, recv = stage
+        peer = lax.rem(here + step + 1, count)
+        return remote(mine.at[pl.ds(base + peer * depth, depth)], inbox.at[step], send.at[0], recv.at[0], group(peer))
+
+    def back_copy(stage, step):
+        group, count, here, base, depth, inbox, send, recv = stage
+        rows = result.at[pl.ds(base + here * depth, depth)]
+        return remote(rows, rows, send.at[1], recv.at[1], group(lax.rem(here + step + 1, count)))
+
+    def all_of(stage, turn):
+        group, count, here, base, depth, inbox, send, recv = stage
+        if turn == 0:
+            block = inbox.at[pl.ds(0, count - 1)]
+        else:
+            block = result.at[pl.ds(0, (count - 1) * depth)]
+        return remote(block, block, send.at[turn], recv.at[turn], sibling)
+
+    def steps(stages):
+        order = [(min(step + 1, stage[1] - step - 1), step, stage) for stage in stages for step in range(stage[1] - 1)]
+        return [(stage, step) for _, step, stage in sorted(order, key=lambda entry: entry[:2])]
+
+    def scatter(stages):
+        for stage, step in steps(stages):
+            scatter_copy(stage, step).start()
+
+    def collect(stages, target):
+        for stage in stages:
+            if stage[1] > 1:
+                all_of(stage, 0).wait_recv()
+            group, count, here, base, depth, inbox, send, recv = stage
+            rows = pl.ds(base + here * depth, depth)
+            total = mine[rows]
+            for step in range(count - 1):
+                total = total + inbox[step]
+            target[rows] = total
+
+    def spread(stages):
+        for stage, step in steps(stages):
+            back_copy(stage, step).start()
+
+    def settle(stages):
+        for stage in stages:
+            if stage[1] > 1:
+                all_of(stage, 1).wait_recv()
+
+    def after_outer():
+        collect(outer, mine)
+        scatter(inner)
+
+    def after_inner():
+        collect(inner, result)
+        spread(inner)
+
+    def after_spread():
+        settle(inner)
+        spread(outer)
+
     probe_pair.wait_recv()
-    mine[...] = probe_buf[...] + terms[core]
-
-    def x_copy(step):
-        peer = x_peers[step]
-        return remote(
-            mine.at[pl.ds(peer * depth_x, depth_x)], x_in.at[step], x_send.at[step], x_recv.at[step], x_ids[step]
-        )
-
-    for step in range(grid_x - 1):
-        x_copy(step).start()
+    for part in range(2):
+        rows = pl.ds(part * PATCH, PATCH)
+        total = probe_buf[rows] + terms[core, rows]
+        for side in range(2):
+            tiles_of = total[:, side * 128 : side * 128 + 128].reshape(PATCH // 8, 8, 128)
+            mine[pl.ds(part * half_tiles + side * PATCH // 8, PATCH // 8)] = tiles_of
+    scatter(outer)
+    put(STRIP, (5, 6, 4, 7))
 
     def chain_copy(way, item):
         return remote(
@@ -324,57 +408,21 @@
             (next_above, next_below)[way],
         )
 
-    own_x = pl.ds(at_x * depth_x, depth_x)
-    own_z = pl.ds(at_x * depth_x + at_z * depth_z, depth_z)
-
-    def z_copy(step):
-        rows = pl.ds(at_x * depth_x + z_peers[step] * depth_z, depth_z)
-        return remote(mine.at[rows], z_in.at[step], z_send.at[step], z_recv.at[step], z_ids[step])
-
-    h_copy = remote(mine.at[own_z], z_in.at[grid_z - 1], h_send, h_recv, h_id)
-
-    def z_back(step, owner):
-        rows = pl.ds(at_x * depth_x + owner * depth_z, depth_z)
-        return remote(probe_ref.at[rows], probe_ref.at[rows], zg_send.at[step], zg_recv.at[step], z_ids[step])
-
-    def x_back(step, owner):
-        rows = pl.ds(owner * depth_x, depth_x)
-        return remote(probe_ref.at[rows], probe_ref.at[rows], xg_send.at[step], xg_recv.at[step], x_ids[step])
-
-    def after_x():
-        for step in range(grid_x - 1):
-            x_copy(step).wait()
-        total = mine[own_x]
-        for step in range(grid_x - 1):
-            total = total + x_in[step]
-        mine[own_x] = total
-        for step in range(grid_z - 1):
-            z_copy(step).start()
-
-    def after_z():
-        for step in range(grid_z - 1):
-            z_copy(step).wait()
-        total = mine[own_z]
-        for step in range(grid_z - 1):
-            total = total + z_in[step]
-        mine[own_z] = total
-        h_copy.start()
-
-    def after_h():
-        h_copy.wait()
-        probe_ref[own_z] = mine[own_z] + z_in[grid_z - 1]
-        for step in range(grid_z - 1):
-            z_back(step, at_z).start()
-
-    def after_z_back():
-        for step in range(grid_z - 1):
-            z_back(step, at_z).wait_send()
-            z_back(step, lax.rem(at_z + grid_z - step - 1, grid_z)).wait_recv()
-        for step in range(grid_x - 1):
-            x_back(step, at_x).start()
+    def first_rows(here):
+        for item in range(4):
+            for way, rank in ranks(here):
+                if rank == 0:
+                    block, half = chain_blocks(way)[item // 2], item % 2
+                    if half == 0:
+                        pair_copy(block).wait_recv()
+                    chain_out[way, item] = pair_buf[half, block] + acc[half, 2 * block + core]
+                    chain_copy(way, item).start()
+
+    by_chip(chip, first_rows)
+    put(0, (3, 0, 2, 1))
 
     def chain_events(here):
-        ready = set()
+        ready = {block for way, rank in ranks(here) if rank == 0 for block in chain_blocks(way)[:2]}
 
         def part(block, half):
             if block not in ready:
@@ -398,11 +446,11 @@
             else:
                 send(way, item, part(blocks[item // 2], half) + chain_in[way, item])
 
-        for item in range(8):
+        for item in range(4, 8):
             for way, rank in ranks(here):
                 if rank == 0:
                     send(way, item, part(chain_blocks(way)[item // 2], item % 2))
-        events = [(8.0, 2, after_x), (13.0, 3, after_z), (16.0, 4, after_h), (20.0, 5, after_z_back)]
+        events = [(9.5, 2, after_outer), (15.5, 3, after_inner), (21.0, 4, after_spread)]
         for way, rank in ranks(here):
             for item, time in timetable(rank).items():
                 events.append((time, way, functools.partial(arrive, way, rank, item)))
@@ -414,31 +462,40 @@
                 result = result + term
             object_ref[half] = result
 
+    def earlier_sends(here):
+        for way, rank in ranks(here):
+            if rank < CHIPS - 1:
+                for slot in range(2):
+                    for cut in range(SUM_CUTS):
+                        sum_copy(way, slot, cut, power).wait_send()
+
+    by_chip(chip, earlier_sends)
+    probe_pair.wait_send()
+    for block in range(8):
+        pair_copy(block).wait_send()
     by_chip(chip, chain_events)
-    for step in range(grid_x - 1):
-        x_back(step, lax.rem(at_x + grid_x - step - 1, grid_x)).wait_recv()
+    settle(outer)
+    for part in range(2):
+        for side in range(2):
+            tiles_of = result[pl.ds(part * half_tiles + side * PATCH // 8, PATCH // 8)]
+            probe_ref[pl.ds(part * PATCH, PATCH), pl.ds(side * 128, 128)] = tiles_of.reshape(PATCH, 128)
 
     def sends(here):
         for way, rank in ranks(here):
             for item in range(10):
                 if item < 4 or rank < stays(item):
                     chain_copy(way, item).wait_send()
-            if rank < CHIPS - 1:
-                for slot in range(2):
-                    for cut in range(SUM_CUTS):
-                        sum_copy(way, slot, cut, power).wait_send()
 
     by_chip(chip, sends)
-    swap.wait_send()
-    probe_pair.wait_send()
-    for cut in range(HALO_CUTS):
-        for way in range(2):
-            halo_copy(way, cut, 0).wait_send()
-            cross_copy(way, cut, core).wait_send()
-    for block in range(8):
-        pair_copy(block).wait_send()
-    for step in range(grid_x - 1):
-        x_back(step, at_x).wait_send()
+    for stage in inner + outer:
+        if stage[1] > 1:
+            all_of(stage, 0).wait_send()
+            all_of(stage, 1).wait_send()
+
+
+def hand_out(object_in, probe_in, object_ref, probe_ref):
+    object_ref[...] = object_in[...]
+    probe_ref[...] = probe_in[...]
 
 
 def chain_blocks(way):
@@ -472,8 +529,7 @@
     grid_z = tiles // 2 // grid_x
     left, right = dft_tables()
     rows = 2 * PATCH
-    depth_x = rows // grid_x
-    depth_z = depth_x // grid_z
+    tile_count = rows * PATCH // (8 * 128)
     block = (2, 32, WIDTH)
     dma = pltpu.SemaphoreType.DMA
 
@@ -505,26 +561,36 @@
                 pltpu.VMEM((2, 10, 32, WIDTH), F32),
                 pltpu.VMEM((2, 10, 32, WIDTH), F32),
                 pltpu.VMEM((rows, PATCH), F32),
-                pltpu.VMEM((rows, PATCH), F32),
-                pltpu.VMEM((grid_x - 1, depth_x, PATCH), F32),
-                pltpu.VMEM((grid_z, depth_z, PATCH), F32),
+                pltpu.VMEM((tile_count, 8, 128), F32),
+                pltpu.VMEM((tile_count, 8, 128), F32),
+                pltpu.VMEM((grid_x, tile_count // 2 // grid_x, 8, 128), F32),
+                pltpu.VMEM((grid_z, tile_count // 2 // grid_z, 8, 128), F32),
+                pltpu.VMEM((2 * grid_z, tile_count // 4 // grid_x // grid_z, 8, 128), F32),
+                pltpu.VMEM((2 * grid_x, tile_count // 4 // grid_x // grid_z, 8, 128), F32),
                 dma((4,)),
                 dma, dma,
                 dma((2, HALO_CUTS)), dma((2, HALO_CUTS)),
-                dma((2, HALO_CUTS)), dma((2, HALO_CUTS)),
+                dma, dma,
                 dma((2, 2 * SUM_CUTS)), dma((2, 2 * SUM_CUTS)),
                 dma((8,)), dma((8,)),
                 dma((2, 10)), dma((2, 10)),
                 dma, dma,
-                dma((grid_x - 1,)), dma((grid_x - 1,)),
-                dma((grid_z,)), dma((grid_z,)),
-                dma, dma,
-                dma((grid_z,)), dma((grid_z,)),
-                dma((grid_x - 1,)), dma((grid_x - 1,)),
+                dma((2,)), dma((2,)),
+                dma((2,)), dma((2,)),
+                dma((2,)), dma((2,)),
+                dma((2,)), dma((2,)),
             ],
             compiler_params=pltpu.CompilerParams(collective_id=0, has_side_effects=True, vmem_limit_bytes=LIMIT),
             name="ptychography",
-        )(object_field, probe_modes, measured, offsets, counts, jnp.asarray(left), jnp.asarray(right))
+        )(object_field, probe_modes, measured, offsets.T, counts, jnp.asarray(left), jnp.asarray(right))
+        object_rows, probe = pl.pallas_call(
+            hand_out,
+            out_shape=(jax.ShapeDtypeStruct(block, F32), jax.ShapeDtypeStruct((rows, PATCH), F32)),
+            in_specs=[VMEM, VMEM],
+            out_specs=(VMEM, VMEM),
+            compiler_params=pltpu.CompilerParams(vmem_limit_bytes=4 * 1024 * 1024),
+            name="hand_out",
+        )(object_rows, probe)
         return object_rows, probe.reshape(1, 2, PATCH, PATCH)
 
     return jax.shard_map(

time: 117 us -> 117 us (level)
  local copies, waits for them, and re-layouts: 4.82 us -> 1.96 us
  Pallas kernels: 110 us -> 112 us
    unnamed x3 -> x4, local copies, waits for them, and re-layouts: 4.82 us -> 1.96 us
    pallas_call x1, Pallas kernels: 110 us -> 111 us  [body(): pl.pallas_call(functools.partial(kernel, tiles, grid_x, grid_z), out_shap...]
where the time goes in v4:
time: 117 us; the launch traced here: 115 us
  Pallas kernels  112 us (96%)
  local copies, waits for them, and re-layouts  1.96 us (2%)
  between operations  1.3 us (1%)
    pallas_call x1, Pallas kernels, body(): pl.pallas_call(functools.partial(kernel, tiles, grid_x, grid_z), out_shap...  111 us

profile of v4, /device:TPU:1, one launch (start us, length us, event | category | flops | bytes accessed | tf_op | source)
XLA Modules:
  0.0 115.4 jit_solution(85198860894532885)
XLA Ops:
  1.3 111.2 %ptychography.1 = (f32[2,32,768]{2,1,0:T(8,128)}, f32[512,256]{1,0:T(8,128)}) custom-call(f32[2,256,768]{2,1,0:T(8,128)} %object_hbm.1, f32[1,2,256,256]{3,2,1,0:T(8,128)} %probe_hbm.1, bf16[4,256,256]{2,1,0:T(8,128)(2,1)} %measured_ref.1, s32[2,4]{1,0:T(2,128)} %bitcast.2, s32[1]{0:T(128)S(6)} %copy.9.counts_ref, bf16[512,1536]{1,0:T(8,128)(2,1)} %constant.4.clone.left_hbm, ...), custom_call_target="tpu_custom_call" | custom-call | tf_op jit(solution)/shard_map/ptychography/pallas_call | solution.py:537
  112.5 0.0 copy-start
  112.5 1.0 copy-done
  113.5 0.0 copy-start.1
  113.5 0.9 copy-done.1
  114.5 0.9 hand_out.1
Async XLA Ops:
  112.5 1.0 copy-start
  113.5 0.9 copy-start.1

commit v5 on v4

--- a/solution.py
+++ b/solution.py
@@ -82,13 +82,13 @@
     return ((0, here), (1, CHIPS - 1 - here))
 
 
-def kernel(tiles, grid_x, grid_z, object_hbm, probe_hbm, measured_ref, offsets_ref, counts_ref, left_hbm, right_hbm,
+def kernel(tiles, grid_x, grid_z, object_hbm, probe_hbm, measured_hbm, offsets_ref, counts_ref, left_hbm, right_hbm,
            object_ref, probe_ref,
-           ext, modes, left, right, windows, far, power, staged, arrived, cut_columns,
+           ext, modes, measured, left, right, windows, far, power, staged, arrived, cut_columns,
            cut_rows, put_columns, put_rows, strips, moved, acc, terms, pair_buf, chain_out,
-           chain_in, probe_buf, mine, result, px_in, qz_in, pz_in, qx_in, local_sem, swap_send, swap_recv, halo_send, halo_recv, cross_send,
-           cross_recv, sum_send, sum_recv, pair_send, pair_recv, chain_send, chain_recv, probe_send, probe_recv, px_send,
-           px_recv, qz_send, qz_recv, pz_send, pz_recv, qx_send, qx_recv):
+           chain_in, probe_buf, mine, result, x_in, z_in, h_in, local_sem, swap_send, swap_recv, halo_send, halo_recv, cross_send,
+           cross_recv, sum_send, sum_recv, pair_send, pair_recv, chain_send, chain_recv, probe_send, probe_recv, x_send,
+           x_recv, z_send, z_recv, h_send, h_recv):
     tile, mode = lax.axis_index("tile"), lax.axis_index("mode")
     chip, core = mode // 2, mode % 2
     high, plane = tile % 2, tile // 2
@@ -107,14 +107,14 @@
     probe_copy = pltpu.make_async_copy(probe_hbm.at[0], modes.at[core], local_sem.at[1])
     left_copy = pltpu.make_async_copy(left_hbm, left, local_sem.at[2])
     right_copy = pltpu.make_async_copy(right_hbm, right, local_sem.at[3])
-    for copy in (own_copy, probe_copy, left_copy, right_copy):
+    measured_copy = pltpu.make_async_copy(measured_hbm.at[pl.ds(2 * core, 2)], measured, local_sem.at[4])
+    for copy in (own_copy, probe_copy, left_copy, right_copy, measured_copy):
         copy.start()
     barrier = pltpu.get_barrier_semaphore()
     friends = [next_above, last_above, next_below, last_below, sibling]
     friends += [at(lax.rem(at_x + step, grid_x), at_z, high) for step in range(1, grid_x)]
-    friends += [at(lax.rem(at_x + step, grid_x), at_z, 1 - high) for step in range(grid_x)]
     friends += [at(at_x, lax.rem(at_z + step, grid_z), high) for step in range(1, grid_z)]
-    friends += [at(at_x, lax.rem(at_z + step, grid_z), 1 - high) for step in range(1, grid_z)]
+    friends += [at(at_x, at_z, 1 - high)]
     for device in friends:
         pl.semaphore_signal(barrier, inc=1, device_id=device, device_id_type=MESH)
     pl.semaphore_wait(barrier, len(friends))
@@ -180,6 +180,7 @@
     swap.wait_recv()
     left_copy.wait()
     right_copy.wait()
+    measured_copy.wait()
     crossed = ext.at[:, pl.ds(STRIP, STRIP // 2)]
     all_across = remote(crossed, crossed, cross_send, cross_recv, sibling)
     all_across.wait_recv()
@@ -256,7 +257,7 @@
 
     def backward(slot):
         index = 2 * core + slot
-        amplitude = jnp.sqrt(measured_ref[index].astype(F32))
+        amplitude = jnp.sqrt(measured[slot].astype(F32))
         live = (index < counts_ref[0]).astype(F32)
         scaling = live * (1.0 - amplitude / jnp.sqrt(jnp.maximum(intensity(slot), 1.0)))
         win_real, win_imag = windows[slot, 0], windows[slot, 1]
@@ -281,6 +282,9 @@
                 terms[pair, pl.ds(PATCH, PATCH)] += probe_imag
                 if pair is not core:
                     probe_pair.start()
+        return sums
+
+    def place(slot, sums):
         for part, term in enumerate(sums):
             for copy, value in enumerate(split(term)):
                 rows = pl.ds((2 * copy + slot) * PATCH, PATCH)
@@ -293,9 +297,9 @@
         for way in range(2):
             halo_copy(way, cut, 0).wait_send()
     by_chip(chip, functools.partial(sum_events, False))
-    backward(0)
+    place(0, backward(0))
     by_chip(chip, functools.partial(sum_events, True))
-    backward(1)
+    sums = backward(1)
 
     def pair_copy(block):
         return remote(
@@ -316,23 +320,12 @@
     def group_z(index):
         return at(at_x, index, high)
 
-    def group_zh(index):
-        return at(at_x, index // 2, index % 2)
-
-    def group_xh(index):
-        return at(index // 2, at_z, index % 2)
-
-    half_tiles = mine.shape[0] // 2
-    x_tiles, z_tiles = half_tiles // grid_x, half_tiles // grid_z
-    outer = (
-        (group_x, grid_x, at_x, 0, x_tiles, px_in, px_send, px_recv),
-        (group_z, grid_z, at_z, half_tiles, z_tiles, qz_in, qz_send, qz_recv),
-    )
-    inner = (
-        (group_zh, 2 * grid_z, 2 * at_z + high, at_x * x_tiles, x_tiles // (2 * grid_z), pz_in, pz_send, pz_recv),
-        (group_xh, 2 * grid_x, 2 * at_x + high, half_tiles + at_z * z_tiles, z_tiles // (2 * grid_x), qx_in, qx_send,
-         qx_recv),
-    )
+    x_tiles = mine.shape[0] // grid_x
+    z_tiles = x_tiles // grid_z
+    over_x = ((group_x, grid_x, at_x, 0, x_tiles, x_in, x_send, x_recv),)
+    over_z = ((group_z, grid_z, at_z, at_x * x_tiles, z_tiles, z_in, z_send, z_recv),)
+    own_tiles = pl.ds(at_x * x_tiles + at_z * z_tiles, z_tiles)
+    h_copy = remote(mine.at[own_tiles], h_in, h_send, h_recv, at(at_x, at_z, 1 - high))
 
     def scatter_copy(stage, step):
         group, count, here, base, depth, inbox, send, recv = stage
@@ -380,17 +373,22 @@
             if stage[1] > 1:
                 all_of(stage, 1).wait_recv()
 
-    def after_outer():
-        collect(outer, mine)
-        scatter(inner)
-
-    def after_inner():
-        collect(inner, result)
-        spread(inner)
-
-    def after_spread():
-        settle(inner)
-        spread(outer)
+    def after_x():
+        collect(over_x, mine)
+        scatter(over_z)
+
+    def after_z():
+        collect(over_z, mine)
+        h_copy.start()
+
+    def after_h():
+        h_copy.wait_recv()
+        result[own_tiles] = mine[own_tiles] + h_in[...]
+        spread(over_z)
+
+    def after_z_back():
+        settle(over_z)
+        spread(over_x)
 
     probe_pair.wait_recv()
     for part in range(2):
@@ -398,8 +396,9 @@
         total = probe_buf[rows] + terms[core, rows]
         for side in range(2):
             tiles_of = total[:, side * 128 : side * 128 + 128].reshape(PATCH // 8, 8, 128)
-            mine[pl.ds(part * half_tiles + side * PATCH // 8, PATCH // 8)] = tiles_of
-    scatter(outer)
+            mine[pl.ds(part * mine.shape[0] // 2 + side * PATCH // 8, PATCH // 8)] = tiles_of
+    scatter(over_x)
+    place(1, sums)
     put(STRIP, (5, 6, 4, 7))
 
     def chain_copy(way, item):
@@ -450,7 +449,7 @@
             for way, rank in ranks(here):
                 if rank == 0:
                     send(way, item, part(chain_blocks(way)[item // 2], item % 2))
-        events = [(9.5, 2, after_outer), (15.5, 3, after_inner), (21.0, 4, after_spread)]
+        events = [(8.0, 2, after_x), (14.0, 3, after_z), (17.0, 4, after_h), (23.0, 5, after_z_back)]
         for way, rank in ranks(here):
             for item, time in timetable(rank).items():
                 events.append((time, way, functools.partial(arrive, way, rank, item)))
@@ -474,12 +473,6 @@
     for block in range(8):
         pair_copy(block).wait_send()
     by_chip(chip, chain_events)
-    settle(outer)
-    for part in range(2):
-        for side in range(2):
-            tiles_of = result[pl.ds(part * half_tiles + side * PATCH // 8, PATCH // 8)]
-            probe_ref[pl.ds(part * PATCH, PATCH), pl.ds(side * 128, 128)] = tiles_of.reshape(PATCH, 128)
-
     def sends(here):
         for way, rank in ranks(here):
             for item in range(10):
@@ -487,7 +480,13 @@
                     chain_copy(way, item).wait_send()
 
     by_chip(chip, sends)
-    for stage in inner + outer:
+    h_copy.wait_send()
+    settle(over_x)
+    for part in range(2):
+        for side in range(2):
+            tiles_of = result[pl.ds(part * mine.shape[0] // 2 + side * PATCH // 8, PATCH // 8)]
+            probe_ref[pl.ds(part * PATCH, PATCH), pl.ds(side * 128, 128)] = tiles_of.reshape(PATCH, 128)
+    for stage in over_z + over_x:
         if stage[1] > 1:
             all_of(stage, 0).wait_send()
             all_of(stage, 1).wait_send()
@@ -537,11 +536,12 @@
         object_rows, probe = pl.pallas_call(
             functools.partial(kernel, tiles, grid_x, grid_z),
             out_shape=(jax.ShapeDtypeStruct(block, F32), jax.ShapeDtypeStruct((rows, PATCH), F32)),
-            in_specs=[ANY, ANY, VMEM, SMEM, SMEM, ANY, ANY],
+            in_specs=[ANY, ANY, ANY, SMEM, SMEM, ANY, ANY],
             out_specs=(VMEM, VMEM),
             scratch_shapes=[
                 pltpu.VMEM((2, 2 * STRIP, WIDTH), F32),
                 pltpu.VMEM((PAIR, 2, PATCH, PATCH), F32),
+                pltpu.VMEM((2, PATCH, PATCH), BF16),
                 pltpu.VMEM(left.shape, BF16),
                 pltpu.VMEM(right.shape, BF16),
                 pltpu.VMEM((2, 2, PATCH, PATCH), F32),
@@ -563,11 +563,10 @@
                 pltpu.VMEM((rows, PATCH), F32),
                 pltpu.VMEM((tile_count, 8, 128), F32),
                 pltpu.VMEM((tile_count, 8, 128), F32),
-                pltpu.VMEM((grid_x, tile_count // 2 // grid_x, 8, 128), F32),
-                pltpu.VMEM((grid_z, tile_count // 2 // grid_z, 8, 128), F32),
-                pltpu.VMEM((2 * grid_z, tile_count // 4 // grid_x // grid_z, 8, 128), F32),
-                pltpu.VMEM((2 * grid_x, tile_count // 4 // grid_x // grid_z, 8, 128), F32),
-                dma((4,)),
+                pltpu.VMEM((grid_x, tile_count // grid_x, 8, 128), F32),
+                pltpu.VMEM((grid_z, tile_count // grid_x // grid_z, 8, 128), F32),
+                pltpu.VMEM((tile_count // grid_x // grid_z, 8, 128), F32),
+                dma((5,)),
                 dma, dma,
                 dma((2, HALO_CUTS)), dma((2, HALO_CUTS)),
                 dma, dma,
@@ -577,8 +576,7 @@
                 dma, dma,
                 dma((2,)), dma((2,)),
                 dma((2,)), dma((2,)),
-                dma((2,)), dma((2,)),
-                dma((2,)), dma((2,)),
+                dma, dma,
             ],
             compiler_params=pltpu.CompilerParams(collective_id=0, has_side_effects=True, vmem_limit_bytes=LIMIT),
             name="ptychography",
@@ -588,7 +586,7 @@
             out_shape=(jax.ShapeDtypeStruct(block, F32), jax.ShapeDtypeStruct((rows, PATCH), F32)),
             in_specs=[VMEM, VMEM],
             out_specs=(VMEM, VMEM),
-            compiler_params=pltpu.CompilerParams(vmem_limit_bytes=4 * 1024 * 1024),
+            compiler_params=pltpu.CompilerParams(vmem_limit_bytes=LIMIT),
             name="hand_out",
         )(object_rows, probe)
         return object_rows, probe.reshape(1, 2, PATCH, PATCH)

time: 117 us -> 111 us (0.949); the launches traced: 115 us -> 111 us
  Pallas kernels: 112 us -> 109 us
  local copies, waits for them, and re-layouts: 1.96 us -> 0 us
    pallas_call x1, Pallas kernels: 111 us -> 107 us  [body(): pl.pallas_call(functools.partial(kernel, tiles, grid_x, grid_z), out_shap...]
    unnamed x4 -> x0, local copies, waits for them, and re-layouts: 1.96 us -> none
where the time goes in v5:
time: 111 us
  Pallas kernels  109 us (98%)
  between operations  1.29 us (1%)
    pallas_call x1, Pallas kernels, body(): pl.pallas_call(functools.partial(kernel, tiles, grid_x, grid_z), out_shap...  107 us

profile of v5, /device:TPU:1, one launch (start us, length us, event | category | flops | bytes accessed | tf_op | source)
XLA Modules:
  0.0 110.6 jit_solution(17486025931206764221)
XLA Ops:
  1.3 107.3 %ptychography.1 = (f32[2,32,768]{2,1,0:T(8,128)}, f32[512,256]{1,0:T(8,128)}) custom-call(f32[2,256,768]{2,1,0:T(8,128)} %object_hbm.1, f32[1,2,256,256]{3,2,1,0:T(8,128)} %probe_hbm.1, bf16[4,256,256]{2,1,0:T(8,128)(2,1)} %measured_hbm.1, s32[2,4]{1,0:T(2,128)} %bitcast.2, s32[1]{0:T(128)S(6)} %copy.9.counts_ref, bf16[512,1536]{1,0:T(8,128)(2,1)} %constant.4.clone.left_hbm, ...), custom_call_target="tpu_custom_call" | custom-call | tf_op jit(solution)/shard_map/ptychography/pallas_call | solution.py:536
  108.6 2.0 %hand_out.1 = (f32[2,32,768]{2,1,0:T(8,128)}, f32[512,256]{1,0:T(8,128)}) custom-call(f32[2,32,768]{2,1,0:T(8,128)} %get-tuple-element.6.object_in, f32[512,256]{1,0:T(8,128)} %get-tuple-element.7.probe_in), custom_call_target="tpu_custom_call" | custom-call | tf_op jit(solution)/shard_map/hand_out/pallas_call | solution.py:584
